TPU v7x, 256 devices: a whole 4x4x8 slice. The times are simulated.
256 devices in a mesh: seq: 128 (over z, x, y_lo, core), tp: 2 (over y_hi).
Axes of the slice: x: 4, y: 4 (y_hi: 2, y_lo: 2; y = y_hi * 2 + y_lo), z: 8, core: 2. Of those that a mesh axis runs over, the one named last changes fastest.
Arguments:
- video_latent: bfloat16 [128, 256, 1152], P('seq'), may hold values from -6 to 6
- shift_temporal: float32 [1152], replicated, may hold values from -3 to 3
- scale_temporal: float32 [1152], replicated, may hold values from -0.5 to 3
- gate_temporal: float32 [1152], replicated, may hold values from 0.4 to 1.6
- temporal_qkv: bfloat16 [1152, 3, 1152], P(None, None, 'tp'), may hold values from -0.1875 to 0.1875
- temporal_proj: bfloat16 [1152, 1152], P('tp'), may hold values from -0.1875 to 0.1875
- cross_query: bfloat16 [1152, 1152], P(None, 'tp'), may hold values from -0.1875 to 0.1875
- cross_kv: bfloat16 [2, 4096, 1152], P(None, 'seq', 'tp'), may hold values from -0.09375 to 0.09375
- cross_proj: bfloat16 [1152, 1152], P('tp'), may hold values from -0.1875 to 0.1875
- text_embed: bfloat16 [300, 4096], P(None, 'seq'), may hold values from -25 to 25, as said below
- text_length: int32 [1], replicated, may hold values from 75 to 300
Outputs:
- block_out: float32 [128, 256, 1152], P('seq')
Inputs may be any that keep to these rules, and one draw needn't show every extreme that they name: `text_embed`: text states, of varied scale over features.
All inputs are finite; a program needn't handle non-finite values.
Results may differ from a plain program's by a relative error of at most 0.025.
Values may be sent and summed in bfloat16 or wider, within the bound.
A program may use at most 128 MiB of HBM per device.

v0:
```python
import jax
import jax.numpy as jnp
from jax import lax
from jax.sharding import PartitionSpec as P

D = 1152
HD = 72


def layer_norm(values):
    center = jnp.mean(values, axis=-1, keepdims=True)
    spread = jnp.mean(jnp.square(values - center), axis=-1, keepdims=True)
    return (values - center) * lax.rsqrt(spread + 1e-06)


def temporal_mix(projected):
    query_rows = projected[:, :, 0]
    key_rows = projected[:, :, 1]
    value_rows = projected[:, :, 2]
    scores = jnp.einsum(
        "flhd,glhd->lhfg", query_rows, key_rows, preferred_element_type=jnp.float32
    ) * HD ** (-0.5)
    weights = jax.nn.softmax(scores, axis=-1).astype(jnp.bfloat16)
    return jnp.einsum(
        "lhfg,glhd->flhd", weights, value_rows, preferred_element_type=jnp.float32
    ).astype(jnp.bfloat16)


def cross_mix(query_rows, key_rows, value_rows, length):
    scores = jnp.einsum(
        "rhd,thd->rht", query_rows.astype(jnp.float32), key_rows, precision=lax.Precision.HIGHEST
    ) * HD ** (-0.5)
    visible = jnp.arange(key_rows.shape[0], dtype=jnp.int32) < length
    scores = jnp.where(visible[None, None, :], scores, -1e30)
    weights = jax.nn.softmax(scores, axis=-1).astype(jnp.bfloat16)
    return jnp.einsum(
        "rht,thd->rhd", weights.astype(jnp.float32), value_rows, precision=lax.Precision.HIGHEST
    ).astype(jnp.bfloat16)


def body(
    video_latent,
    shift_temporal,
    scale_temporal,
    gate_temporal,
    temporal_qkv,
    temporal_proj,
    cross_query,
    cross_kv,
    cross_proj,
    text_embed,
    text_length,
):
    locations = video_latent.shape[1]
    columns = temporal_proj.shape[0]
    local_heads = columns // HD
    frames = lax.axis_size("seq") * video_latent.shape[0]
    tokens_f = video_latent.reshape(locations, D).astype(jnp.float32)
    normed = (layer_norm(tokens_f) * (1.0 + scale_temporal) + shift_temporal).astype(jnp.bfloat16)
    qkv_flat = temporal_qkv.reshape(D, 3 * columns)
    projected = jnp.dot(normed, qkv_flat, preferred_element_type=jnp.float32).astype(jnp.bfloat16)
    projected = projected.reshape(1, locations, 3, local_heads, HD)
    attended = temporal_mix(
        lax.all_to_all(projected, "seq", split_axis=1, concat_axis=0, tiled=True)
    )
    attended = attended.reshape(frames, -1, columns)
    returned = lax.all_to_all(attended, "seq", split_axis=0, concat_axis=1, tiled=True)
    returned = returned.reshape(locations, columns)
    temporal_part = jnp.dot(returned, temporal_proj, preferred_element_type=jnp.float32)
    temporal_out = lax.psum(temporal_part.astype(jnp.bfloat16), "tp").astype(jnp.float32)
    mixed = tokens_f + gate_temporal * temporal_out
    text_count = text_embed.shape[0]
    text_kv = jnp.einsum(
        "tr,krc->ktc",
        lax.all_gather(text_embed, "seq", axis=1, tiled=True),
        lax.all_gather(cross_kv, "seq", axis=1, tiled=True),
        preferred_element_type=jnp.float32,
    )
    text_kv = text_kv.reshape(2, text_count, local_heads, HD)
    mixed_in = mixed.astype(jnp.bfloat16)
    query_rows = jnp.dot(mixed_in, cross_query, preferred_element_type=jnp.float32).astype(
        jnp.bfloat16
    )
    crossed = cross_mix(
        query_rows.reshape(locations, local_heads, HD), text_kv[0], text_kv[1], text_length[0]
    )
    crossed = crossed.reshape(locations, columns)
    cross_part = jnp.dot(crossed, cross_proj, preferred_element_type=jnp.float32)
    cross_out = lax.psum(cross_part.astype(jnp.bfloat16), "tp").astype(jnp.float32)
    block_out = mixed + cross_out
    return block_out.reshape(1, locations, D)


def solution(mesh):
    return jax.shard_map(
        body,
        mesh=mesh,
        in_specs=(
            P("seq", None, None),
            P(),
            P(),
            P(),
            P(None, None, "tp"),
            P("tp", None),
            P(None, "tp"),
            P(None, "seq", "tp"),
            P("tp", None),
            P(None, "seq"),
            P(),
        ),
        out_specs=P("seq", None, None),
        check_vma=False,
    )
```

profile of v0, /device:TPU:1, one launch (start us, length us, event | category | flops | bytes accessed | tf_op | source)
XLA Modules:
  0.0 614.8 jit_solution(10537010168607638386)
XLA Ops:
  7.4 0.0 copy-start
  7.4 0.0 all-reduce.3.cloned.1.call-start
  7.4 0.8 broadcast_add_fusion
  8.2 1.2 convert_reduce_fusion
  9.4 1.4 fusion.21
  10.8 4.7 convolution_convert_fusion
  15.5 1.9 copy.23
  17.4 54.2 %all_to_all.21 = bf16[1,256,3,8,72]{4,3,2,0,1:T(8,128)(2,1)S(1)} all-to-all(bf16[1,256,3,8,72]{4,3,2,0,1:T(8,128)(2,1)S(1)} %copy.23), channel_id=1, replica_groups=mesh['seq'=128,'tp'=2] {'seq'}, dimensions={1} | all-to-all | bytes 1769472 | tf_op jit(solution)/shard_map/all_to_all | solution.py:64
  71.5 0.3 fusion.46
  71.8 0.5 copy.34
  72.3 0.5 copy.33
  72.7 0.5 fusion.48
  73.3 1.3 convolution_multiply_fusion
  74.6 0.5 copy.32
  75.0 2.1 convolution_convert_fusion.4
  77.1 0.8 copy.28
  77.9 22.5 %all_to_all.22 = bf16[128,2,576]{2,1,0:T(2,128)(2,1)S(1)} all-to-all(bf16[128,2,576]{2,1,0:T(2,128)(2,1)S(1)} %copy.28), channel_id=1, replica_groups=mesh['seq'=128,'tp'=2] {'seq'}, dimensions={0} | all-to-all | bytes 589824 | tf_op jit(solution)/shard_map/all_to_all | solution.py:67
  100.4 0.2 reshape.88
  100.6 0.0 copy-done
  100.6 0.0 copy-start.1
  100.6 0.0 copy-start.4
  100.6 1.5 convolution_convert_fusion.2
  102.1 0.0 all-reduce.3.cloned.1.call-update
  102.1 0.0 all-gather.5.cloned.1.call-start
  102.2 0.5 all-gather.5.cloned.1.call-update
  102.7 0.0 all-gather.3.cloned.1.call-start
  102.8 0.5 all-gather.3.cloned.1.call-update
  103.3 0.2 all-reduce.5.cloned.1.call-start
  104.2 37.1 %all-reduce.3.cloned.1.call-done = bf16[256,1152]{1,0:T(8,128)(2,1)} async-done(((bf16[256,1152]{1,0:T(8,128)(2,1)}), bf16[256,1152]{1,0:T(8,128)(2,1)}) %all-reduce.3.cloned.1.call-update) | async-done | bytes 589840 | tf_op jit(solution)/shard_map/psum | solution.py:70
  141.2 0.0 copy-done.1
  141.3 0.0 copy-done.4
  141.3 2.1 convolution_convert_fusion.3
  143.4 173.8 %all-gather.5.cloned.1.call-done = bf16[300,4096]{0,1:T(8,128)(2,1)} async-done(((bf16[300,32]{0,1:T(8,128)(2,1)}), bf16[300,4096]{0,1:T(8,128)(2,1)}) %all-gather.5.cloned.1.call-update) | async-done | bytes 2457616 | tf_op jit(solution)/shard_map/all_gather | solution.py:75
  317.2 227.7 %all-gather.3.cloned.1.call-done = bf16[2,4096,576]{2,1,0:T(8,128)(2,1)} async-done(((bf16[2,32,576]{2,1,0:T(8,128)(2,1)}), bf16[2,4096,576]{2,1,0:T(8,128)(2,1)}) %all-gather.3.cloned.1.call-update) | async-done | bytes 9437200 | tf_op jit(solution)/shard_map/all_gather | solution.py:76
  544.8 7.8 %fusion.9 = f32[2,300,576]{2,1,0:T(8,128)S(1)} fusion(bf16[2,4096,576]{2,1,0:T(8,128)(2,1)} %all-gather.3.cloned.1.call-done, bf16[300,4096]{0,1:T(8,128)(2,1)} %all-gather.5.cloned.1.call-done), kind=kOutput, calls=%fused_computation.17 | convolution fusion | flops 2831155200 | bytes 13277184 | tf_op jit(solution)/shard_map/tr,krc->ktc/dot_general | solution.py:73
  552.6 1.0 fusion.47
  553.6 1.2 copy.29
  554.8 1.4 copy.30
  556.3 1.3 fusion.54
  557.5 0.0 copy-start.2
  557.6 0.9 fusion.53
  558.4 0.3 copy-done.2
  558.7 0.0 copy-start.5
  558.7 1.0 fusion.19
  559.7 0.3 copy-done.5
  560.0 0.0 copy-start.3
  560.0 1.5 convolution_convert_fusion.1
  561.6 0.0 all-reduce.5.cloned.1.call-update
  561.6 43.5 %all-reduce.5.cloned.1.call-done = bf16[256,1152]{1,0:T(8,128)(2,1)} async-done(((bf16[256,1152]{1,0:T(8,128)(2,1)}), bf16[256,1152]{1,0:T(8,128)(2,1)}) %all-reduce.5.cloned.1.call-update) | async-done | bytes 589840 | tf_op jit(solution)/shard_map/psum | solution.py:89
  605.1 0.0 copy-done.3
  605.1 2.3 add_bitcast_fusion
  (3 shorter events, 0.0 us)
Async XLA Ops:
  7.4 93.2 %copy-start = (bf16[576,1152]{1,0:T(8,128)(2,1)S(1)}, bf16[576,1152]{1,0:T(8,128)(2,1)}, u32[]{:S(2)}) copy-start(bf16[576,1152]{1,0:T(8,128)(2,1)} %param.16) | copy-start | bytes 3981316
  7.4 133.9 %all-reduce.3.cloned.1.call-start = ((), (), s32[]{:S(2)}) async-start(), calls=%async_computation.2 | async-start | bytes 1179648 | tf_op jit(solution)/shard_map/psum | solution.py:70
  100.6 40.6 %copy-start.1 = (bf16[1,256,1152]{2,1,0:T(8,128)(2,1)S(1)}, bf16[1,256,1152]{2,1,0:T(8,128)(2,1)}, u32[]{:S(2)}) copy-start(bf16[1,256,1152]{2,1,0:T(8,128)(2,1)} %param.11) | copy-start | bytes 1769476
  100.6 40.6 %copy-start.4 = (f32[1152]{0:T(1024)S(1)}, f32[1152]{0:T(1024)}, u32[]{:S(2)}) copy-start(f32[1152]{0:T(1024)} %param.14) | copy-start | bytes 13828
  102.1 215.1 %all-gather.5.cloned.1.call-start = ((), (), s32[]{:S(2)}) async-start(), calls=%async_computation.4 | async-start | bytes 3170304 | tf_op jit(solution)/shard_map/all_gather | solution.py:75
  102.7 442.1 %all-gather.3.cloned.1.call-start = ((), (), s32[]{:S(2)}) async-start(), calls=%async_computation.3 | async-start | bytes 10567680 | tf_op jit(solution)/shard_map/all_gather | solution.py:76
  103.3 501.8 %all-reduce.5.cloned.1.call-start = ((), (), s32[]{:S(2)}) async-start(), calls=%async_computation.5 | async-start | bytes 1179648 | tf_op jit(solution)/shard_map/psum | solution.py:89
  557.5 1.2 copy-start.2
  558.7 1.3 copy-start.5
  560.0 45.1 %copy-start.3 = (bf16[256,1152]{1,0:T(8,128)(2,1)S(1)}, bf16[256,1152]{1,0:T(8,128)(2,1)}, u32[]{:S(2)}) copy-start(bf16[256,1152]{1,0:T(8,128)(2,1)} %all-reduce.3.cloned.1.call-done) | copy-start | bytes 1769476
Sparse Core Ops, SparseCore 0:
  102.3 38.9 all-reduce.2
  561.7 43.3 all-reduce.4
Sparse Core Ops, SparseCore 1:
  104.6 212.5 all-gather.4
  319.0 225.8 all-gather.2
where the time goes:
time: 615 us
  waiting for transfers between devices  483 us (79%)
  blocking collectives  76.6 us (12%)
  matrix products  23.7 us (4%)
  between operations  15.6 us (3%)
  local copies, waits for them, and re-layouts  8.84 us (1%)
  other arithmetic  6.59 us (1%)
    all_gather x1, waiting for transfers between devices, body(): lax.all_gather(cross_kv, 'seq', axis=1, tiled=True)  228 us
    all_gather x1, waiting for transfers between devices, body(): lax.all_gather(text_embed, 'seq', axis=1, tiled=True)  174 us
    all_to_all x1, blocking collectives, body(): lax.all_to_all(projected, 'seq', split_axis=1, concat_axis=0, tiled=True)  54.2 us
    psum x1, waiting for transfers between devices, body(): lax.psum(cross_part.astype(jnp.bfloat16), 'tp').astype(jnp.float32)  43.5 us
    psum x1, waiting for transfers between devices, body(): lax.psum(temporal_part.astype(jnp.bfloat16), 'tp').astype(jnp.float32)  37.1 us
    all_to_all x1, blocking collectives, body(): lax.all_to_all(attended, 'seq', split_axis=0, concat_axis=1, tiled=True)  22.5 us
  transfers between devices with their start and end apart: 4, of which 4 were waited for; matrix products, arithmetic and copies ran while one was open for 0% of the time, Pallas kernels for 0%

commit v1 on v0

v1 whole, which is shorter than its diff:
```python
import jax
import jax.numpy as jnp
from jax import lax
from jax.experimental import pallas as pl
from jax.experimental.pallas import tpu as pltpu
from jax.sharding import PartitionSpec as P

D = 1152
HD = 72
HEADS = 8
WIDTH = HEADS * HD
TOKENS = 256
NZ = 8
NQ = 16
TEXT_ROWS = 304
EXP_SCALE = HD ** (-0.5) * 1.4426950408889634
MESH = pl.DeviceIdType.MESH


def rows_of(index, size):
    return pl.ds(pl.multiple_of(index * size, size), size)


def attend(query, key, value, visible, store):
    tiles = [None] * 5
    for head in range(HEADS):
        low, high = head * HD, (head + 1) * HD
        first, last = low // 128, (high - 1) // 128
        start, end = first * 128, min((last + 1) * 128, WIDTH)
        rows = query[:, start:end]
        lane = lax.broadcasted_iota(jnp.int32, rows.shape, 1) + start
        rows = jnp.where((lane >= low) & (lane < high), rows, jnp.zeros_like(rows))
        scores = lax.dot_general(
            rows, key[:, start:end], (((1,), (1,)), ((), ())), preferred_element_type=jnp.float32
        )
        scores = jnp.where(visible, scores, -1e30)
        top = jnp.max(scores, axis=-1, keepdims=True)
        weights = jnp.exp2((scores - top) * EXP_SCALE)
        total = jnp.sum(weights, axis=-1, keepdims=True)
        mixed = jnp.dot(
            weights.astype(jnp.bfloat16), value[:, start:end], preferred_element_type=jnp.float32
        ) * (1.0 / total)
        for tile in range(first, last + 1):
            piece = mixed[:, tile * 128 - start : min((tile + 1) * 128, WIDTH) - start]
            if tiles[tile] is not None:
                lane = lax.broadcasted_iota(jnp.int32, piece.shape, 1) + tile * 128
                piece = jnp.where(lane >= low, piece, tiles[tile])
            tiles[tile] = piece
            if high >= min((tile + 1) * 128, WIDTH):
                store(tile, piece.astype(jnp.bfloat16))


def kernel(
    length_ref, x_ref, shift_ref, scale_ref, gate_ref, wqkv_hbm, wp_hbm, wcq_hbm, wcp_hbm, tk_ref, tv_ref,
    out_ref,
    wqkv, wp, wp_far, wcq, wcp, wcp_far,
    s1, t32, msg, xin, normed, qkv, att, att_far, branch, o2, om, o1,
    load_sem, w_send, w_recv, s1_send, s1_recv, s2_send, s2_recv,
    a_send, a_recv, o2_send, o2_recv, o1_send, o1_recv,
):
    seq, hi = lax.axis_index("seq"), lax.axis_index("tp")
    z, q = seq // NQ, lax.rem(seq, NQ)
    core, spot = lax.rem(q, 2), q // 2

    def other_y(index):
        return index + 2 - 4 * lax.rem(index // 2, 2)

    def group_of(index):
        return index + hi * (other_y(index) - index)

    def place_of(index):
        group = group_of(index)
        return lax.rem(group, 2) * 8 + group // 2

    def at_z(index):
        return (index * NQ + q, hi)

    def at_q(index):
        return (z * NQ + index, hi)

    pair = (z * NQ + other_y(q), 1 - hi)
    sibling = at_q(q + 1 - 2 * core)

    loads = [
        pltpu.make_async_copy(source, target, load_sem.at[n])
        for n, (source, target) in enumerate(
            ((wqkv_hbm, wqkv), (wp_hbm, wp), (wcq_hbm, wcq), (wcp_hbm, wcp))
        )
    ]
    for load in loads:
        load.start()

    barrier = pltpu.get_barrier_semaphore()
    for step in range(1, NZ):
        pl.semaphore_signal(barrier, inc=1, device_id=at_z(lax.rem(z + step, NZ)), device_id_type=MESH)
    for step in range(1, NQ):
        pl.semaphore_signal(barrier, inc=1, device_id=at_q(lax.rem(q + step, NQ)), device_id_type=MESH)
    pl.semaphore_signal(barrier, inc=1, device_id=pair, device_id_type=MESH)
    pl.semaphore_wait(barrier, NZ - 1 + NQ - 1 + 1)

    def remote(source, target, send, recv, device):
        return pltpu.make_async_remote_copy(
            src_ref=source, dst_ref=target, send_sem=send, recv_sem=recv, device_id=device, device_id_type=MESH
        )

    sent = []

    for half in range(2):
        for n, step in enumerate((4, 3, 5, 2, 6, 1, 7)):
            target = lax.rem(z + step, NZ)
            copy = remote(
                x_ref.at[pl.ds(pl.multiple_of(target * 32 + half * 16, 16), 16)],
                s1.at[z, half], s1_send.at[n, half], s1_recv.at[z, half], at_z(target),
            )
            copy.start()
            sent.append(copy)
    half_rows = pl.ds(pl.multiple_of(core * 288, 288), 288)
    for n, (source, target) in enumerate(((wp_hbm, wp_far), (wcp_hbm, wcp_far))):
        copy = remote(source.at[half_rows], target.at[half_rows], w_send.at[n], w_recv.at[n], pair)
        copy.start()
        sent.append(copy)
    for half in range(2):
        s1[z, half] = x_ref[pl.ds(pl.multiple_of(z * 32 + half * 16, 16), 16)]

    for half in range(2):
        for step in range(1, NZ):
            source = lax.rem(z + step, NZ)
            remote(s1.at[source, half], s1.at[source, half], s1_send.at[0, half], s1_recv.at[source, half], at_z(source)).wait_recv()
        def spread_in(tile, carry):
            lanes = pl.ds(pl.multiple_of(tile * 128, 128), 128)
            for n in range(NZ):
                t32[n * 16 : (n + 1) * 16] = s1[n, half, :, lanes].astype(jnp.float32)
            for n in range(8):
                first = t32[pl.ds(2 * n, 8, stride=16), :]
                second = t32[pl.ds(2 * n + 1, 8, stride=16), :]
                msg[half * 8 + n, :, lanes] = jnp.concatenate([first, second], axis=0).astype(jnp.bfloat16)
            return carry

        lax.fori_loop(0, D // 128, spread_in, 0)
        for step in range(8):
            dest = 2 * lax.rem(spot + step, 8) + half
            copy = remote(msg.at[place_of(dest)], xin.at[q], s2_send.at[half * 8 + step], s2_recv.at[q], at_q(dest))
            if step:
                copy.start()
            else:
                pl.when(core != half)(copy.start)
            sent.append((copy, core != half) if step == 0 else copy)
    xin[q] = msg[place_of(q)]
    for step in range(1, NQ):
        source = lax.rem(q + step, NQ)
        remote(xin.at[source], xin.at[source], s2_send.at[0], s2_recv.at[source], at_q(source)).wait_recv()

    def norm_rows(n, carry):
        values = xin[n].astype(jnp.float32)
        center = jnp.mean(values, axis=-1, keepdims=True)
        values = values - center
        spread = jnp.mean(jnp.square(values), axis=-1, keepdims=True)
        values = values * lax.rsqrt(spread + 1e-06) * (1.0 + scale_ref[...]) + shift_ref[...]
        normed[rows_of(n, 16)] = values.astype(jnp.bfloat16)
        return carry

    lax.fori_loop(0, NQ, norm_rows, 0)
    loads[0].wait()

    def project(n, carry):
        qkv[n] = jnp.dot(normed[...], wqkv[n], preferred_element_type=jnp.float32).astype(jnp.bfloat16)
        return carry

    lax.fori_loop(0, 3, project, 0)

    for n, target in enumerate((wp_far, wcp_far)):
        remote(target.at[half_rows], target.at[half_rows], w_send.at[n], w_recv.at[n], pair).wait_recv()
        copy = remote(target.at[half_rows], target.at[half_rows], w_send.at[2 + n], w_recv.at[2 + n], sibling)
        copy.start()
        sent.append(copy)

    row = lax.broadcasted_iota(jnp.int32, (TOKENS, TOKENS), 0)
    column = lax.broadcasted_iota(jnp.int32, (TOKENS, TOKENS), 1)
    same = lax.rem(row // 8, 2) == lax.rem(column // 8, 2)

    def put(target):
        def store(tile, piece):
            target[:, tile * 128 : tile * 128 + piece.shape[1]] = piece

        return store

    attend(qkv.at[0], qkv.at[1], qkv.at[2], same, put(att.at[0]))
    swap = remote(att.at[0], att_far.at[0], a_send.at[0], a_recv.at[0], pair)
    swap.start()
    sent.append(swap)
    loads[1].wait()
    branch[...] = jnp.dot(att[0], wp[...], preferred_element_type=jnp.float32)
    other_rows = pl.ds(pl.multiple_of(288 - core * 288, 288), 288)
    remote(wp_far.at[other_rows], wp_far.at[other_rows], w_send.at[2], w_recv.at[2], sibling).wait_recv()
    swap.wait_recv()
    branch[...] = (branch[...] + jnp.dot(att_far[0], wp_far[...], preferred_element_type=jnp.float32)) * gate_ref[...]

    def mix_rows(n, carry):
        rows = rows_of(n, 16)
        normed[rows] = (xin[n].astype(jnp.float32) + branch[rows]).astype(jnp.bfloat16)
        return carry

    lax.fori_loop(0, NQ, mix_rows, 0)
    loads[2].wait()
    qkv[0] = jnp.dot(normed[...], wcq[...], preferred_element_type=jnp.float32).astype(jnp.bfloat16)
    text = lax.broadcasted_iota(jnp.int32, (1, TEXT_ROWS), 1)
    attend(qkv.at[0], tk_ref, tv_ref, text < length_ref[0], put(att.at[1]))
    swap = remote(att.at[1], att_far.at[1], a_send.at[1], a_recv.at[1], pair)
    swap.start()
    sent.append(swap)
    loads[3].wait()
    branch[...] += jnp.dot(att[1], wcp[...], preferred_element_type=jnp.float32)
    remote(wcp_far.at[other_rows], wcp_far.at[other_rows], w_send.at[3], w_recv.at[3], sibling).wait_recv()
    swap.wait_recv()
    branch[...] += jnp.dot(att_far[1], wcp_far[...], preferred_element_type=jnp.float32)

    def drain():
        for copy in sent:
            if isinstance(copy, tuple):
                pl.when(copy[1])(copy[0].wait_send)
            else:
                copy.wait_send()
        sent.clear()

    drain()

    for n in range(NQ):
        om[n] = branch[n * 16 : (n + 1) * 16].astype(jnp.bfloat16)
    place = place_of(q)
    for step in range(1, NQ):
        dest = lax.rem(q + step, NQ)
        copy = remote(
            om.at[dest], o2.at[place], o2_send.at[step], o2_recv.at[place], at_q(dest),
        )
        copy.start()
        sent.append(copy)
    o2[place] = om[q]
    for half in range(2):
        for step in range(8):
            source = 2 * lax.rem(spot + step, 8) + half
            slot = place_of(source)
            copy = remote(o2.at[slot], o2.at[slot], o2_send.at[0], o2_recv.at[slot], at_q(source))
            if step:
                copy.wait_recv()
            else:
                pl.when(core != half)(copy.wait_recv)
        def spread_out(tile, carry):
            lanes = pl.ds(pl.multiple_of(tile * 128, 128), 128)
            for n in range(8):
                t32[n * 16 : (n + 1) * 16] = o2[half * 8 + n, :, lanes].astype(jnp.float32)
            for n in range(NZ):
                msg[2 * n + half, :, lanes] = t32[pl.ds(n, 16, stride=8), :].astype(jnp.bfloat16)
            return carry

        lax.fori_loop(0, D // 128, spread_out, 0)
        for n, step in enumerate((4, 3, 5, 2, 6, 1, 7)):
            target = lax.rem(z + step, NZ)
            copy = remote(
                msg.at[2 * target + half], o1.at[2 * z + half], o1_send.at[n, half], o1_recv.at[z, half], at_z(target)
            )
            copy.start()
            sent.append(copy)
        o1[2 * z + half] = msg[2 * z + half]
    for half in range(2):
        for step in range(1, NZ):
            source = lax.rem(z + step, NZ)
            remote(o1.at[2 * source + half], o1.at[2 * source + half], o1_send.at[0, half], o1_recv.at[source, half], at_z(source)).wait_recv()

    def finish(n, carry):
        rows = rows_of(n, 16)
        out_ref[rows] = x_ref[rows].astype(jnp.float32) + o1[n].astype(jnp.float32)
        return carry

    lax.fori_loop(0, NQ, finish, 0)
    drain()


def mega(length, x, shift, scale, gate, wqkv, wp, wcq, wcp, tk, tv):
    vmem = pl.BlockSpec(memory_space=pltpu.VMEM)
    hbm = pl.BlockSpec(memory_space=pl.ANY)
    bf16, f32 = jnp.bfloat16, jnp.float32
    dma = pltpu.SemaphoreType.DMA
    return pl.pallas_call(
        kernel,
        out_shape=jax.ShapeDtypeStruct((TOKENS, D), f32),
        in_specs=[pl.BlockSpec(memory_space=pltpu.SMEM), vmem, vmem, vmem, vmem, hbm, hbm, hbm, hbm, vmem, vmem],
        out_specs=vmem,
        scratch_shapes=[
            pltpu.VMEM((3, D, WIDTH), bf16),
            pltpu.VMEM((WIDTH, D), bf16),
            pltpu.VMEM((WIDTH, D), bf16),
            pltpu.VMEM((D, WIDTH), bf16),
            pltpu.VMEM((WIDTH, D), bf16),
            pltpu.VMEM((WIDTH, D), bf16),
            pltpu.VMEM((NZ, 2, 16, D), bf16),
            pltpu.VMEM((128, 128), f32),
            pltpu.VMEM((16, 16, D), bf16),
            pltpu.VMEM((16, 16, D), bf16),
            pltpu.VMEM((TOKENS, D), bf16),
            pltpu.VMEM((3, TOKENS, WIDTH), bf16),
            pltpu.VMEM((2, TOKENS, WIDTH), bf16),
            pltpu.VMEM((2, TOKENS, WIDTH), bf16),
            pltpu.VMEM((TOKENS, D), f32),
            pltpu.VMEM((16, 16, D), bf16),
            pltpu.VMEM((16, 16, D), bf16),
            pltpu.VMEM((16, 16, D), bf16),
            dma((4,)), dma((4,)), dma((4,)),
            dma((7, 2)), dma((8, 2)), dma((16,)), dma((16,)),
            dma((2,)), dma((2,)), dma((16,)), dma((16,)), dma((7, 2)), dma((8, 2)),
        ],
        compiler_params=pltpu.CompilerParams(
            collective_id=0, has_side_effects=True, vmem_limit_bytes=48 * 1024 * 1024
        ),
        cost_estimate=pl.CostEstimate(flops=4_000_000_000, bytes_accessed=12_000_000, transcendentals=2_000_000),
        name="stdit",
    )(length, x, shift, scale, gate, wqkv, wp, wcq, wcp, tk, tv)


def body(
    video_latent, shift_temporal, scale_temporal, gate_temporal, temporal_qkv, temporal_proj,
    cross_query, cross_kv, cross_proj, text_embed, text_length,
):
    partial = jnp.einsum("tr,krc->ktc", text_embed, cross_kv, preferred_element_type=jnp.float32)
    text_kv = lax.psum(partial, "seq").astype(jnp.bfloat16)
    text_kv = jnp.pad(text_kv, ((0, 0), (0, TEXT_ROWS - text_kv.shape[1]), (0, 0)))
    out = mega(
        text_length, video_latent.reshape(TOKENS, D),
        shift_temporal.reshape(1, D), scale_temporal.reshape(1, D), gate_temporal.reshape(1, D),
        jnp.transpose(temporal_qkv, (1, 0, 2)), temporal_proj, cross_query, cross_proj, text_kv[0], text_kv[1],
    )
    return out.reshape(1, TOKENS, D)


def solution(mesh):
    return jax.shard_map(
        body,
        mesh=mesh,
        in_specs=(
            P("seq", None, None), P(), P(), P(), P(None, None, "tp"), P("tp", None), P(None, "tp"),
            P(None, "seq", "tp"), P("tp", None), P(None, "seq"), P(),
        ),
        out_specs=P("seq", None, None),
        check_vma=False,
    )
```

time: 615 us -> 662 us (1.076)
  blocking collectives: 76.6 us -> 563 us
  waiting for transfers between devices: 483 us -> 0 us
  Pallas kernels: 0 us -> 82.8 us
  matrix products: 23.7 us -> 0.41 us
  between operations: 15.6 us -> 0.74 us
    psum x0 -> x1, blocking collectives: none -> 563 us  [body(): text_kv = lax.psum(partial, 'seq').astype(jnp.bfloat16)]
    all_gather x2 -> x0, waiting for transfers between devices: 401 us -> none  [the longest x1 228 us: body(): lax.all_gather(cross_kv, 'seq', axis=1, tiled=True)]
    pallas_call x0 -> x1, Pallas kernels: none -> 82.8 us  [mega(): pl.pallas_call(kernel, out_shape=jax.ShapeDtypeStruct((TOKENS, D), f32),...]
    psum x2 -> x0, waiting for transfers between devices: 80.6 us -> none  [the longest x1 43.5 us: body(): lax.psum(cross_part.astype(jnp.bfloat16), 'tp').astype(jnp.float32)]
    all_to_all x2 -> x0, blocking collectives: 76.6 us -> none  [the longest x1 54.2 us: body(): lax.all_to_all(projected, 'seq', split_axis=1, concat_axis=0, tiled=True)]
    dot_general x9 -> x1, matrix products: 23.2 us -> 0.41 us  [body(): jnp.einsum('tr,krc->ktc', text_embed, cross_kv, preferred_element_type=jn...]
    unnamed x15 -> x13, local copies, waits for them, and re-layouts: 2.04 us -> 11.4 us
  transfers between devices with their start and end apart: 4 -> 0, of which waited for: 4 -> 0; matrix products, arithmetic and copies ran while one was open for 0% -> 0% of each run, Pallas kernels for 0% -> 0%
where the time goes in v1:
time: 662 us; the launch traced here: 661 us
  blocking collectives  563 us (85%)
  Pallas kernels  82.8 us (13%)
  local copies, waits for them, and re-layouts  13.6 us (2%)
    psum x1, blocking collectives, body(): text_kv = lax.psum(partial, 'seq').astype(jnp.bfloat16)  563 us
    pallas_call x1, Pallas kernels, mega(): pl.pallas_call(kernel, out_shape=jax.ShapeDtypeStruct((TOKENS, D), f32),...  82.8 us

profile of v1, /device:TPU:1, one launch (start us, length us, event | category | flops | bytes accessed | tf_op | source)
XLA Modules:
  0.0 661.1 jit_solution(16399458181020425786)
XLA Ops:
  0.0 0.0 copy-start
  0.0 0.0 copy-start.4
  0.7 0.7 reshape.16.shift_ref
  1.4 0.7 reshape.17.scale_ref
  2.1 0.7 reshape.18.gate_ref
  2.8 2.6 copy.13.wcq_hbm
  5.4 0.0 copy-done
  5.4 0.0 copy-done.4
  5.4 0.4 convolution_bitcast_fusion
  5.8 563.5 %all-reduce.2 = bf16[2,300,576]{2,1,0:T(8,128)(2,1)S(1)} all-reduce(f32[2,300,576]{2,1,0:T(8,128)S(1)} %convolution_bitcast_fusion), channel_id=1, replica_groups=mesh['seq'=128,'tp'=2] {'seq'}, use_global_device_ids=true, to_apply=%region_0.0 | all-reduce | flops 345600 | bytes 2073600 | tf_op jit(solution)/shard_map/psum | solution.py:324
  569.3 0.1 fusion.1
  569.4 0.0 copy-start.1
  569.4 0.0 copy-start.2
  569.4 6.7 %copy.12 = bf16[1152,3,576]{2,0,1:T(8,128)(2,1)} copy(bf16[1152,3,576]{0,2,1:T(8,128)(2,1)} %param.15) | data formatting | bytes 7962624 | tf_op args[4]
  576.1 0.0 copy-done.1
  576.1 0.0 copy-done.2
  576.2 0.0 copy-start.3
  576.2 1.1 copy-done.3
  577.2 82.8 %stdit.1 = f32[256,1152]{1,0:T(8,128)S(1)} custom-call(s32[1]{0:T(128)S(6)} %copy.17.length_ref, bf16[256,1152]{1,0:T(8,128)(2,1)S(1)} %bitcast.14, f32[1,1152]{1,0:T(1,128)S(1)} %reshape.16.shift_ref, f32[1,1152]{1,0:T(1,128)S(1)} %reshape.17.scale_ref, f32[1,1152]{1,0:T(1,128)S(1)} %reshape.18.gate_ref, bf16[3,1152,576]{2,1,0:T(8,128)(2,1)} %bitcast.15, ...), custom_call_target="tpu_custom_call" | custom-call | flops 4000000000 | bytes 12000000 | tf_op jit(solution)/shard_map/stdit/pallas_call | solution.py:283
  660.1 1.0 copy.18
Async XLA Ops:
  0.0 5.4 copy-start
  0.0 5.4 copy-start.4
  569.4 6.7 %copy-start.1 = (bf16[576,1152]{1,0:T(8,128)(2,1)S(1)}, bf16[576,1152]{1,0:T(8,128)(2,1)}, u32[]{:S(2)}) copy-start(bf16[576,1152]{1,0:T(8,128)(2,1)} %wp_hbm.1) | copy-start | bytes 3981316
  569.4 6.7 %copy-start.2 = (bf16[576,1152]{1,0:T(8,128)(2,1)S(1)}, bf16[576,1152]{1,0:T(8,128)(2,1)}, u32[]{:S(2)}) copy-start(bf16[576,1152]{1,0:T(8,128)(2,1)} %wcp_hbm.1) | copy-start | bytes 3981316
  576.2 1.1 copy-start.3

commit v2 on v1

--- a/solution.py
+++ b/solution.py
@@ -12,6 +12,7 @@
 TOKENS = 256
 NZ = 8
 NQ = 16
+TEXT_LEN = 300
 TEXT_ROWS = 304
 EXP_SCALE = HD ** (-0.5) * 1.4426950408889634
 MESH = pl.DeviceIdType.MESH
@@ -50,13 +51,21 @@
                 store(tile, piece.astype(jnp.bfloat16))
 
 
+def across(rows, weights):
+    return lax.dot_general(
+        rows, weights, (((1,), (1,)), ((), ())), preferred_element_type=jnp.float32
+    ).astype(jnp.bfloat16)
+
+
 def kernel(
-    length_ref, x_ref, shift_ref, scale_ref, gate_ref, wqkv_hbm, wp_hbm, wcq_hbm, wcp_hbm, tk_ref, tv_ref,
+    length_ref, x_ref, shift_ref, scale_ref, gate_ref, wqkv_hbm, wp_hbm, wcq_hbm, wcp_hbm, ckv_ref, te_ref,
     out_ref,
     wqkv, wp, wp_far, wcq, wcp, wcp_far,
     s1, t32, msg, xin, normed, qkv, att, att_far, branch, o2, om, o1,
+    te_pad, part, core_in, part_x, x_in, part_z, z_in, part_y, y_in, full, tk, tv,
     load_sem, w_send, w_recv, s1_send, s1_recv, s2_send, s2_recv,
     a_send, a_recv, o2_send, o2_recv, o1_send, o1_recv,
+    c_send, c_recv, x_send, x_recv, z_send, z_recv, y_send, y_recv,
 ):
     seq, hi = lax.axis_index("seq"), lax.axis_index("tp")
     z, q = seq // NQ, lax.rem(seq, NQ)
@@ -78,6 +87,10 @@
     def at_q(index):
         return (z * NQ + index, hi)
 
+    def at_x(index):
+        return at_q(index * 4 + lax.rem(q, 4))
+
+    x = q // 4
     pair = (z * NQ + other_y(q), 1 - hi)
     sibling = at_q(q + 1 - 2 * core)
 
@@ -104,6 +117,85 @@
         )
 
     sent = []
+
+    def send(source, target, send_sem, recv_sem, device):
+        copy = remote(source, target, send_sem, recv_sem, device)
+        copy.start()
+        sent.append(copy)
+
+    def arrived(target, recv_sem, device):
+        remote(target, target, c_send.at[0], recv_sem, device).wait_recv()
+
+    def text_products():
+        te_pad[...] = jnp.zeros_like(te_pad)
+        te_pad[:, :TEXT_LEN] = te_ref[...]
+        part[190:] = jnp.zeros((2, 16, 128), jnp.bfloat16)
+        for which in range(2):
+            product = lax.dot_general(
+                te_pad[:, :TEXT_ROWS], ckv_ref[which], (((0,), (0,)), ((), ())), preferred_element_type=jnp.float32
+            ).astype(jnp.bfloat16)
+            product = jnp.concatenate([product, jnp.zeros((TEXT_ROWS, 64), jnp.bfloat16)], axis=1)
+            for r in range(TEXT_ROWS // 16):
+                for tile in range(5):
+                    part[r * 10 + which * 5 + tile] = product[r * 16 : r * 16 + 16, tile * 128 : tile * 128 + 128]
+        send(part.at[pl.ds(96 - 96 * core, 96)], core_in, c_send.at[0], c_recv.at[0], sibling)
+
+    def text_core_sum():
+        arrived(core_in, c_recv.at[0], sibling)
+        part_x[...] = (part[pl.ds(96 * core, 96)].astype(jnp.float32) + core_in[...].astype(jnp.float32)).astype(jnp.bfloat16)
+        for step in range(1, 4):
+            target = lax.rem(x + step, 4)
+            send(part_x.at[pl.ds(24 * target, 24)], x_in.at[x], x_send.at[0, step], x_recv.at[0, x], at_x(target))
+
+    def text_x_sum():
+        total = part_x[pl.ds(24 * x, 24)].astype(jnp.float32)
+        for step in range(1, 4):
+            source = lax.rem(x + step, 4)
+            arrived(x_in.at[source], x_recv.at[0, source], at_x(source))
+            total += x_in[source].astype(jnp.float32)
+        part_z[...] = total.astype(jnp.bfloat16)
+        for step in range(1, NZ):
+            target = lax.rem(z + step, NZ)
+            send(part_z.at[pl.ds(3 * target, 3)], z_in.at[z], z_send.at[0, step], z_recv.at[0, z], at_z(target))
+
+    def text_z_sum():
+        total = part_z[pl.ds(3 * z, 3)].astype(jnp.float32)
+        for step in range(1, NZ):
+            source = lax.rem(z + step, NZ)
+            arrived(z_in.at[source], z_recv.at[0, source], at_z(source))
+            total += z_in[source].astype(jnp.float32)
+        part_y[...] = total.astype(jnp.bfloat16)
+        send(part_y, y_in, y_send.at[0], y_recv.at[0], at_q(other_y(q)))
+
+    def text_y_sum():
+        arrived(y_in, y_recv.at[0], at_q(other_y(q)))
+        mine = full.at[pl.ds(96 * core + 24 * x + 3 * z, 3)]
+        mine[...] = (part_y[...].astype(jnp.float32) + y_in[...].astype(jnp.float32)).astype(jnp.bfloat16)
+        for step in range(1, NZ):
+            send(mine, mine, z_send.at[1, step], z_recv.at[1, z], at_z(lax.rem(z + step, NZ)))
+
+    def text_z_gather():
+        for step in range(1, NZ):
+            source = lax.rem(z + step, NZ)
+            arrived(full.at[pl.ds(96 * core + 24 * x + 3 * source, 3)], z_recv.at[1, source], at_z(source))
+        mine = full.at[pl.ds(96 * core + 24 * x, 24)]
+        for step in range(1, 4):
+            send(mine, mine, x_send.at[1, step], x_recv.at[1, x], at_x(lax.rem(x + step, 4)))
+
+    def text_x_gather():
+        for step in range(1, 4):
+            source = lax.rem(x + step, 4)
+            arrived(full.at[pl.ds(96 * core + 24 * source, 24)], x_recv.at[1, source], at_x(source))
+        mine = full.at[pl.ds(96 * core, 96)]
+        send(mine, mine, c_send.at[1], c_recv.at[1], sibling)
+
+    def text_core_gather():
+        arrived(full.at[pl.ds(96 - 96 * core, 96)], c_recv.at[1], sibling)
+        for which, target in enumerate((tk, tv)):
+            for r in range(TEXT_ROWS // 16):
+                for tile in range(5):
+                    width = min(128, WIDTH - tile * 128)
+                    target[r * 16 : r * 16 + 16, tile * 128 : tile * 128 + width] = full[r * 10 + which * 5 + tile][:, :width]
 
     for half in range(2):
         for n, step in enumerate((4, 3, 5, 2, 6, 1, 7)):
@@ -122,6 +214,8 @@
     for half in range(2):
         s1[z, half] = x_ref[pl.ds(pl.multiple_of(z * 32 + half * 16, 16), 16)]
 
+    text_products()
+
     for half in range(2):
         for step in range(1, NZ):
             source = lax.rem(z + step, NZ)
@@ -145,6 +239,10 @@
             else:
                 pl.when(core != half)(copy.start)
             sent.append((copy, core != half) if step == 0 else copy)
+        if half:
+            text_x_sum()
+        else:
+            text_core_sum()
     xin[q] = msg[place_of(q)]
     for step in range(1, NQ):
         source = lax.rem(q + step, NQ)
@@ -163,10 +261,12 @@
     loads[0].wait()
 
     def project(n, carry):
-        qkv[n] = jnp.dot(normed[...], wqkv[n], preferred_element_type=jnp.float32).astype(jnp.bfloat16)
+        qkv[n] = across(normed[...], wqkv[n])
         return carry
 
     lax.fori_loop(0, 3, project, 0)
+
+    text_z_sum()
 
     for n, target in enumerate((wp_far, wcp_far)):
         remote(target.at[half_rows], target.at[half_rows], w_send.at[n], w_recv.at[n], pair).wait_recv()
@@ -188,10 +288,12 @@
     swap = remote(att.at[0], att_far.at[0], a_send.at[0], a_recv.at[0], pair)
     swap.start()
     sent.append(swap)
+    text_y_sum()
     loads[1].wait()
     branch[...] = jnp.dot(att[0], wp[...], preferred_element_type=jnp.float32)
     other_rows = pl.ds(pl.multiple_of(288 - core * 288, 288), 288)
     remote(wp_far.at[other_rows], wp_far.at[other_rows], w_send.at[2], w_recv.at[2], sibling).wait_recv()
+    text_z_gather()
     swap.wait_recv()
     branch[...] = (branch[...] + jnp.dot(att_far[0], wp_far[...], preferred_element_type=jnp.float32)) * gate_ref[...]
 
@@ -201,10 +303,12 @@
         return carry
 
     lax.fori_loop(0, NQ, mix_rows, 0)
+    text_x_gather()
     loads[2].wait()
-    qkv[0] = jnp.dot(normed[...], wcq[...], preferred_element_type=jnp.float32).astype(jnp.bfloat16)
+    qkv[0] = across(normed[...], wcq[...])
+    text_core_gather()
     text = lax.broadcasted_iota(jnp.int32, (1, TEXT_ROWS), 1)
-    attend(qkv.at[0], tk_ref, tv_ref, text < length_ref[0], put(att.at[1]))
+    attend(qkv.at[0], tk, tv, text < length_ref[0], put(att.at[1]))
     swap = remote(att.at[1], att_far.at[1], a_send.at[1], a_recv.at[1], pair)
     swap.start()
     sent.append(swap)
@@ -275,7 +379,7 @@
     drain()
 
 
-def mega(length, x, shift, scale, gate, wqkv, wp, wcq, wcp, tk, tv):
+def mega(length, x, shift, scale, gate, wqkv, wp, wcq, wcp, ckv, te):
     vmem = pl.BlockSpec(memory_space=pltpu.VMEM)
     hbm = pl.BlockSpec(memory_space=pl.ANY)
     bf16, f32 = jnp.bfloat16, jnp.float32
@@ -286,10 +390,10 @@
         in_specs=[pl.BlockSpec(memory_space=pltpu.SMEM), vmem, vmem, vmem, vmem, hbm, hbm, hbm, hbm, vmem, vmem],
         out_specs=vmem,
         scratch_shapes=[
-            pltpu.VMEM((3, D, WIDTH), bf16),
+            pltpu.VMEM((3, WIDTH, D), bf16),
             pltpu.VMEM((WIDTH, D), bf16),
             pltpu.VMEM((WIDTH, D), bf16),
-            pltpu.VMEM((D, WIDTH), bf16),
+            pltpu.VMEM((WIDTH, D), bf16),
             pltpu.VMEM((WIDTH, D), bf16),
             pltpu.VMEM((WIDTH, D), bf16),
             pltpu.VMEM((NZ, 2, 16, D), bf16),
@@ -304,29 +408,39 @@
             pltpu.VMEM((16, 16, D), bf16),
             pltpu.VMEM((16, 16, D), bf16),
             pltpu.VMEM((16, 16, D), bf16),
+            pltpu.VMEM((32, 384), bf16),
+            pltpu.VMEM((192, 16, 128), bf16),
+            pltpu.VMEM((96, 16, 128), bf16),
+            pltpu.VMEM((96, 16, 128), bf16),
+            pltpu.VMEM((4, 24, 16, 128), bf16),
+            pltpu.VMEM((24, 16, 128), bf16),
+            pltpu.VMEM((8, 3, 16, 128), bf16),
+            pltpu.VMEM((3, 16, 128), bf16),
+            pltpu.VMEM((3, 16, 128), bf16),
+            pltpu.VMEM((192, 16, 128), bf16),
+            pltpu.VMEM((TEXT_ROWS, WIDTH), bf16),
+            pltpu.VMEM((TEXT_ROWS, WIDTH), bf16),
             dma((4,)), dma((4,)), dma((4,)),
             dma((7, 2)), dma((8, 2)), dma((16,)), dma((16,)),
             dma((2,)), dma((2,)), dma((16,)), dma((16,)), dma((7, 2)), dma((8, 2)),
+            dma((2,)), dma((2,)), dma((2, 4)), dma((2, 4)), dma((2, 8)), dma((2, 8)), dma((1,)), dma((1,)),
         ],
         compiler_params=pltpu.CompilerParams(
             collective_id=0, has_side_effects=True, vmem_limit_bytes=48 * 1024 * 1024
         ),
         cost_estimate=pl.CostEstimate(flops=4_000_000_000, bytes_accessed=12_000_000, transcendentals=2_000_000),
         name="stdit",
-    )(length, x, shift, scale, gate, wqkv, wp, wcq, wcp, tk, tv)
+    )(length, x, shift, scale, gate, wqkv, wp, wcq, wcp, ckv, te)
 
 
 def body(
     video_latent, shift_temporal, scale_temporal, gate_temporal, temporal_qkv, temporal_proj,
     cross_query, cross_kv, cross_proj, text_embed, text_length,
 ):
-    partial = jnp.einsum("tr,krc->ktc", text_embed, cross_kv, preferred_element_type=jnp.float32)
-    text_kv = lax.psum(partial, "seq").astype(jnp.bfloat16)
-    text_kv = jnp.pad(text_kv, ((0, 0), (0, TEXT_ROWS - text_kv.shape[1]), (0, 0)))
     out = mega(
         text_length, video_latent.reshape(TOKENS, D),
         shift_temporal.reshape(1, D), scale_temporal.reshape(1, D), gate_temporal.reshape(1, D),
-        jnp.transpose(temporal_qkv, (1, 0, 2)), temporal_proj, cross_query, cross_proj, text_kv[0], text_kv[1],
+        jnp.transpose(temporal_qkv, (1, 2, 0)), temporal_proj, cross_query.T, cross_proj, cross_kv, text_embed.T,
     )
     return out.reshape(1, TOKENS, D)
 

time: 662 us -> 102 us (0.15)
  blocking collectives: 563 us -> 0 us
  Pallas kernels: 82.8 us -> 90.8 us
    psum x1 -> x0, blocking collectives: 563 us -> none  [body(): text_kv = lax.psum(partial, 'seq').astype(jnp.bfloat16)]
    pallas_call x1, Pallas kernels: 82.8 us -> 90.8 us  [mega(): pl.pallas_call(kernel, out_shape=jax.ShapeDtypeStruct((TOKENS, D), f32),...]
where the time goes in v2:
time: 102 us; the launch traced here: 101 us
  Pallas kernels  90.8 us (89%)
  local copies, waits for them, and re-layouts  9.77 us (10%)
    pallas_call x1, Pallas kernels, mega(): pl.pallas_call(kernel, out_shape=jax.ShapeDtypeStruct((TOKENS, D), f32),...  90.8 us
    unnamed x13, local copies, waits for them, and re-layouts  7.67 us

profile of v2, /device:TPU:1, one launch (start us, length us, event | category | flops | bytes accessed | tf_op | source)
XLA Modules:
  0.0 101.3 jit_solution(1616655289007230351)
XLA Ops:
  0.7 0.7 reshape.16.shift_ref
  1.4 0.7 reshape.17.scale_ref
  2.1 0.7 reshape.18.gate_ref
  2.8 0.0 copy-start
  2.8 1.3 %copy-done = bf16[576,1152]{1,0:T(8,128)(2,1)S(1)} copy-done((bf16[576,1152]{1,0:T(8,128)(2,1)S(1)}, bf16[576,1152]{1,0:T(8,128)(2,1)}, u32[]{:S(2)}) %copy-start) | copy-done | bytes 1327128
  4.1 0.0 copy-start.1
  4.1 1.3 %copy-done.1 = bf16[1152,576]{0,1:T(8,128)(2,1)S(1)} copy-done((bf16[1152,576]{0,1:T(8,128)(2,1)S(1)}, bf16[1152,576]{0,1:T(8,128)(2,1)}, u32[]{:S(2)}) %copy-start.1) | copy-done | bytes 1327128
  5.4 0.0 copy-start.2
  5.4 1.3 %copy-done.2 = bf16[576,1152]{1,0:T(8,128)(2,1)S(1)} copy-done((bf16[576,1152]{1,0:T(8,128)(2,1)S(1)}, bf16[576,1152]{1,0:T(8,128)(2,1)}, u32[]{:S(2)}) %copy-start.2) | copy-done | bytes 1327128
  6.7 0.0 copy-start.3
  6.7 1.1 %copy-done.3 = bf16[1,256,1152]{2,1,0:T(8,128)(2,1)S(1)} copy-done((bf16[1,256,1152]{2,1,0:T(8,128)(2,1)S(1)}, bf16[1,256,1152]{2,1,0:T(8,128)(2,1)}, u32[]{:S(2)}) %copy-start.3) | copy-done | bytes 589848
  7.8 0.0 copy-start.4
  7.8 0.9 copy-done.4
  8.7 0.0 copy-start.5
  8.7 0.7 copy-done.5
  9.4 90.8 %stdit.1 = f32[256,1152]{1,0:T(8,128)S(1)} custom-call(s32[1]{0:T(128)S(6)} %copy.13.length_ref, bf16[256,1152]{1,0:T(8,128)(2,1)S(1)} %bitcast.7, f32[1,1152]{1,0:T(1,128)S(1)} %reshape.16.shift_ref, f32[1,1152]{1,0:T(1,128)S(1)} %reshape.17.scale_ref, f32[1,1152]{1,0:T(1,128)S(1)} %reshape.18.gate_ref, bf16[3,576,1152]{2,1,0:T(8,128)(2,1)} %bitcast.9, ...), custom_call_target="tpu_custom_call" | custom-call | flops 4000000000 | bytes 12000000 | tf_op jit(solution)/shard_map/stdit/pallas_call | solution.py:387
  100.2 1.0 %copy.14 = f32[1,256,1152]{2,1,0:T(8,128)} copy(f32[1,256,1152]{2,1,0:T(8,128)S(1)} %bitcast.5) | data formatting | bytes 2359296
Async XLA Ops:
  2.8 1.3 %copy-start = (bf16[576,1152]{1,0:T(8,128)(2,1)S(1)}, bf16[576,1152]{1,0:T(8,128)(2,1)}, u32[]{:S(2)}) copy-start(bf16[576,1152]{1,0:T(8,128)(2,1)} %wp_hbm.1) | copy-start | bytes 3981316
  4.1 1.3 %copy-start.1 = (bf16[1152,576]{0,1:T(8,128)(2,1)S(1)}, bf16[1152,576]{0,1:T(8,128)(2,1)}, u32[]{:S(2)}) copy-start(bf16[1152,576]{0,1:T(8,128)(2,1)} %param.17) | copy-start | bytes 3981316
  5.4 1.3 %copy-start.2 = (bf16[576,1152]{1,0:T(8,128)(2,1)S(1)}, bf16[576,1152]{1,0:T(8,128)(2,1)}, u32[]{:S(2)}) copy-start(bf16[576,1152]{1,0:T(8,128)(2,1)} %wcp_hbm.1) | copy-start | bytes 3981316
  6.7 1.1 %copy-start.3 = (bf16[1,256,1152]{2,1,0:T(8,128)(2,1)S(1)}, bf16[1,256,1152]{2,1,0:T(8,128)(2,1)}, u32[]{:S(2)}) copy-start(bf16[1,256,1152]{2,1,0:T(8,128)(2,1)} %param.11) | copy-start | bytes 1769476
  7.8 0.9 copy-start.4
  8.7 0.7 copy-start.5

commit v3 on v2

--- a/solution.py
+++ b/solution.py
@@ -58,9 +58,9 @@
 
 
 def kernel(
-    length_ref, x_ref, shift_ref, scale_ref, gate_ref, wqkv_hbm, wp_hbm, wcq_hbm, wcp_hbm, ckv_ref, te_ref,
+    length_ref, x_hbm, shift_hbm, scale_hbm, gate_hbm, wqkv_hbm, wp_hbm, wcq_hbm, wcp_hbm, ckv_hbm, te_hbm,
     out_ref,
-    wqkv, wp, wp_far, wcq, wcp, wcp_far,
+    x_ref, shift_ref, scale_ref, gate_ref, ckv_ref, te_ref, wqkv, wp, wp_far, wcq, wcp, wcp_far,
     s1, t32, msg, xin, normed, qkv, att, att_far, branch, o2, om, o1,
     te_pad, part, core_in, part_x, x_in, part_z, z_in, part_y, y_in, full, tk, tv,
     load_sem, w_send, w_recv, s1_send, s1_recv, s2_send, s2_recv,
@@ -97,7 +97,10 @@
     loads = [
         pltpu.make_async_copy(source, target, load_sem.at[n])
         for n, (source, target) in enumerate(
-            ((wqkv_hbm, wqkv), (wp_hbm, wp), (wcq_hbm, wcq), (wcp_hbm, wcp))
+            (
+                (wqkv_hbm, wqkv), (wp_hbm, wp), (wcq_hbm, wcq), (wcp_hbm, wcp), (x_hbm, x_ref),
+                (shift_hbm, shift_ref), (scale_hbm, scale_ref), (gate_hbm, gate_ref), (ckv_hbm, ckv_ref), (te_hbm, te_ref),
+            )
         )
     ]
     for load in loads:
@@ -118,15 +121,32 @@
 
     sent = []
 
-    def send(source, target, send_sem, recv_sem, device):
+    def send(source, target, send_sem, recv_sem, device, when=None):
         copy = remote(source, target, send_sem, recv_sem, device)
-        copy.start()
-        sent.append(copy)
-
-    def arrived(target, recv_sem, device):
-        remote(target, target, c_send.at[0], recv_sem, device).wait_recv()
+        if when is None:
+            copy.start()
+        else:
+            pl.when(when)(copy.start)
+        sent.append((copy, when))
+
+    def arrived(target, recv_sem, device, when=None):
+        copy = remote(target, target, c_send.at[0], recv_sem, device)
+        if when is None:
+            copy.wait_recv()
+        else:
+            pl.when(when)(copy.wait_recv)
+
+    def drain():
+        for copy, when in sent:
+            if when is None:
+                copy.wait_send()
+            else:
+                pl.when(when)(copy.wait_send)
+        sent.clear()
 
     def text_products():
+        loads[8].wait()
+        loads[9].wait()
         te_pad[...] = jnp.zeros_like(te_pad)
         te_pad[:, :TEXT_LEN] = te_ref[...]
         part[190:] = jnp.zeros((2, 16, 128), jnp.bfloat16)
@@ -200,26 +220,22 @@
     for half in range(2):
         for n, step in enumerate((4, 3, 5, 2, 6, 1, 7)):
             target = lax.rem(z + step, NZ)
-            copy = remote(
-                x_ref.at[pl.ds(pl.multiple_of(target * 32 + half * 16, 16), 16)],
+            send(
+                x_hbm.at[pl.ds(pl.multiple_of(target * 32 + half * 16, 16), 16)],
                 s1.at[z, half], s1_send.at[n, half], s1_recv.at[z, half], at_z(target),
             )
-            copy.start()
-            sent.append(copy)
     half_rows = pl.ds(pl.multiple_of(core * 288, 288), 288)
     for n, (source, target) in enumerate(((wp_hbm, wp_far), (wcp_hbm, wcp_far))):
-        copy = remote(source.at[half_rows], target.at[half_rows], w_send.at[n], w_recv.at[n], pair)
-        copy.start()
-        sent.append(copy)
+        send(source.at[half_rows], target.at[half_rows], w_send.at[n], w_recv.at[n], pair)
+    loads[4].wait()
     for half in range(2):
         s1[z, half] = x_ref[pl.ds(pl.multiple_of(z * 32 + half * 16, 16), 16)]
-
     text_products()
 
     for half in range(2):
         for step in range(1, NZ):
             source = lax.rem(z + step, NZ)
-            remote(s1.at[source, half], s1.at[source, half], s1_send.at[0, half], s1_recv.at[source, half], at_z(source)).wait_recv()
+            arrived(s1.at[source, half], s1_recv.at[source, half], at_z(source))
         def spread_in(tile, carry):
             lanes = pl.ds(pl.multiple_of(tile * 128, 128), 128)
             for n in range(NZ):
@@ -233,12 +249,8 @@
         lax.fori_loop(0, D // 128, spread_in, 0)
         for step in range(8):
             dest = 2 * lax.rem(spot + step, 8) + half
-            copy = remote(msg.at[place_of(dest)], xin.at[q], s2_send.at[half * 8 + step], s2_recv.at[q], at_q(dest))
-            if step:
-                copy.start()
-            else:
-                pl.when(core != half)(copy.start)
-            sent.append((copy, core != half) if step == 0 else copy)
+            when = None if step else core != half
+            send(msg.at[place_of(dest)], xin.at[q], s2_send.at[half * 8 + step], s2_recv.at[q], at_q(dest), when)
         if half:
             text_x_sum()
         else:
@@ -246,14 +258,17 @@
     xin[q] = msg[place_of(q)]
     for step in range(1, NQ):
         source = lax.rem(q + step, NQ)
-        remote(xin.at[source], xin.at[source], s2_send.at[0], s2_recv.at[source], at_q(source)).wait_recv()
+        arrived(xin.at[source], s2_recv.at[source], at_q(source))
+
+    for n in (5, 6, 7):
+        loads[n].wait()
 
     def norm_rows(n, carry):
         values = xin[n].astype(jnp.float32)
         center = jnp.mean(values, axis=-1, keepdims=True)
         values = values - center
         spread = jnp.mean(jnp.square(values), axis=-1, keepdims=True)
-        values = values * lax.rsqrt(spread + 1e-06) * (1.0 + scale_ref[...]) + shift_ref[...]
+        values = values * lax.rsqrt(spread + 1e-06) * (1.0 + scale_ref[...].reshape(1, D)) + shift_ref[...].reshape(1, D)
         normed[rows_of(n, 16)] = values.astype(jnp.bfloat16)
         return carry
 
@@ -269,10 +284,8 @@
     text_z_sum()
 
     for n, target in enumerate((wp_far, wcp_far)):
-        remote(target.at[half_rows], target.at[half_rows], w_send.at[n], w_recv.at[n], pair).wait_recv()
-        copy = remote(target.at[half_rows], target.at[half_rows], w_send.at[2 + n], w_recv.at[2 + n], sibling)
-        copy.start()
-        sent.append(copy)
+        arrived(target.at[half_rows], w_recv.at[n], pair)
+        send(target.at[half_rows], target.at[half_rows], w_send.at[2 + n], w_recv.at[2 + n], sibling)
 
     row = lax.broadcasted_iota(jnp.int32, (TOKENS, TOKENS), 0)
     column = lax.broadcasted_iota(jnp.int32, (TOKENS, TOKENS), 1)
@@ -285,17 +298,15 @@
         return store
 
     attend(qkv.at[0], qkv.at[1], qkv.at[2], same, put(att.at[0]))
-    swap = remote(att.at[0], att_far.at[0], a_send.at[0], a_recv.at[0], pair)
-    swap.start()
-    sent.append(swap)
+    send(att.at[0], att_far.at[0], a_send.at[0], a_recv.at[0], pair)
     text_y_sum()
     loads[1].wait()
     branch[...] = jnp.dot(att[0], wp[...], preferred_element_type=jnp.float32)
     other_rows = pl.ds(pl.multiple_of(288 - core * 288, 288), 288)
-    remote(wp_far.at[other_rows], wp_far.at[other_rows], w_send.at[2], w_recv.at[2], sibling).wait_recv()
+    arrived(wp_far.at[other_rows], w_recv.at[2], sibling)
     text_z_gather()
-    swap.wait_recv()
-    branch[...] = (branch[...] + jnp.dot(att_far[0], wp_far[...], preferred_element_type=jnp.float32)) * gate_ref[...]
+    arrived(att_far.at[0], a_recv.at[0], pair)
+    branch[...] = (branch[...] + jnp.dot(att_far[0], wp_far[...], preferred_element_type=jnp.float32)) * gate_ref[...].reshape(1, D)
 
     def mix_rows(n, carry):
         rows = rows_of(n, 16)
@@ -309,22 +320,12 @@
     text_core_gather()
     text = lax.broadcasted_iota(jnp.int32, (1, TEXT_ROWS), 1)
     attend(qkv.at[0], tk, tv, text < length_ref[0], put(att.at[1]))
-    swap = remote(att.at[1], att_far.at[1], a_send.at[1], a_recv.at[1], pair)
-    swap.start()
-    sent.append(swap)
+    send(att.at[1], att_far.at[1], a_send.at[1], a_recv.at[1], pair)
     loads[3].wait()
     branch[...] += jnp.dot(att[1], wcp[...], preferred_element_type=jnp.float32)
-    remote(wcp_far.at[other_rows], wcp_far.at[other_rows], w_send.at[3], w_recv.at[3], sibling).wait_recv()
-    swap.wait_recv()
+    arrived(wcp_far.at[other_rows], w_recv.at[3], sibling)
+    arrived(att_far.at[1], a_recv.at[1], pair)
     branch[...] += jnp.dot(att_far[1], wcp_far[...], preferred_element_type=jnp.float32)
-
-    def drain():
-        for copy in sent:
-            if isinstance(copy, tuple):
-                pl.when(copy[1])(copy[0].wait_send)
-            else:
-                copy.wait_send()
-        sent.clear()
 
     drain()
 
@@ -333,21 +334,13 @@
     place = place_of(q)
     for step in range(1, NQ):
         dest = lax.rem(q + step, NQ)
-        copy = remote(
-            om.at[dest], o2.at[place], o2_send.at[step], o2_recv.at[place], at_q(dest),
-        )
-        copy.start()
-        sent.append(copy)
+        send(om.at[dest], o2.at[place], o2_send.at[step], o2_recv.at[place], at_q(dest))
     o2[place] = om[q]
     for half in range(2):
         for step in range(8):
             source = 2 * lax.rem(spot + step, 8) + half
             slot = place_of(source)
-            copy = remote(o2.at[slot], o2.at[slot], o2_send.at[0], o2_recv.at[slot], at_q(source))
-            if step:
-                copy.wait_recv()
-            else:
-                pl.when(core != half)(copy.wait_recv)
+            arrived(o2.at[slot], o2_recv.at[slot], at_q(source), None if step else core != half)
         def spread_out(tile, carry):
             lanes = pl.ds(pl.multiple_of(tile * 128, 128), 128)
             for n in range(8):
@@ -359,16 +352,14 @@
         lax.fori_loop(0, D // 128, spread_out, 0)
         for n, step in enumerate((4, 3, 5, 2, 6, 1, 7)):
             target = lax.rem(z + step, NZ)
-            copy = remote(
+            send(
                 msg.at[2 * target + half], o1.at[2 * z + half], o1_send.at[n, half], o1_recv.at[z, half], at_z(target)
             )
-            copy.start()
-            sent.append(copy)
         o1[2 * z + half] = msg[2 * z + half]
     for half in range(2):
         for step in range(1, NZ):
             source = lax.rem(z + step, NZ)
-            remote(o1.at[2 * source + half], o1.at[2 * source + half], o1_send.at[0, half], o1_recv.at[source, half], at_z(source)).wait_recv()
+            arrived(o1.at[2 * source + half], o1_recv.at[source, half], at_z(source))
 
     def finish(n, carry):
         rows = rows_of(n, 16)
@@ -381,15 +372,21 @@
 
 def mega(length, x, shift, scale, gate, wqkv, wp, wcq, wcp, ckv, te):
     vmem = pl.BlockSpec(memory_space=pltpu.VMEM)
-    hbm = pl.BlockSpec(memory_space=pl.ANY)
+    hbm = pl.BlockSpec(memory_space=pltpu.HBM)
     bf16, f32 = jnp.bfloat16, jnp.float32
     dma = pltpu.SemaphoreType.DMA
     return pl.pallas_call(
         kernel,
         out_shape=jax.ShapeDtypeStruct((TOKENS, D), f32),
-        in_specs=[pl.BlockSpec(memory_space=pltpu.SMEM), vmem, vmem, vmem, vmem, hbm, hbm, hbm, hbm, vmem, vmem],
+        in_specs=[pl.BlockSpec(memory_space=pltpu.SMEM)] + [hbm] * 10,
         out_specs=vmem,
         scratch_shapes=[
+            pltpu.VMEM((TOKENS, D), bf16),
+            pltpu.VMEM((D,), f32),
+            pltpu.VMEM((D,), f32),
+            pltpu.VMEM((D,), f32),
+            pltpu.VMEM((2, 32, WIDTH), bf16),
+            pltpu.VMEM((32, TEXT_LEN), bf16),
             pltpu.VMEM((3, WIDTH, D), bf16),
             pltpu.VMEM((WIDTH, D), bf16),
             pltpu.VMEM((WIDTH, D), bf16),
@@ -420,13 +417,13 @@
             pltpu.VMEM((192, 16, 128), bf16),
             pltpu.VMEM((TEXT_ROWS, WIDTH), bf16),
             pltpu.VMEM((TEXT_ROWS, WIDTH), bf16),
-            dma((4,)), dma((4,)), dma((4,)),
+            dma((10,)), dma((4,)), dma((4,)),
             dma((7, 2)), dma((8, 2)), dma((16,)), dma((16,)),
             dma((2,)), dma((2,)), dma((16,)), dma((16,)), dma((7, 2)), dma((8, 2)),
             dma((2,)), dma((2,)), dma((2, 4)), dma((2, 4)), dma((2, 8)), dma((2, 8)), dma((1,)), dma((1,)),
         ],
         compiler_params=pltpu.CompilerParams(
-            collective_id=0, has_side_effects=True, vmem_limit_bytes=48 * 1024 * 1024
+            collective_id=0, has_side_effects=True, vmem_limit_bytes=60 * 1024 * 1024
         ),
         cost_estimate=pl.CostEstimate(flops=4_000_000_000, bytes_accessed=12_000_000, transcendentals=2_000_000),
         name="stdit",
@@ -439,7 +436,7 @@
 ):
     out = mega(
         text_length, video_latent.reshape(TOKENS, D),
-        shift_temporal.reshape(1, D), scale_temporal.reshape(1, D), gate_temporal.reshape(1, D),
+        shift_temporal, scale_temporal, gate_temporal,
         jnp.transpose(temporal_qkv, (1, 2, 0)), temporal_proj, cross_query.T, cross_proj, cross_kv, text_embed.T,
     )
     return out.reshape(1, TOKENS, D)

time: 102 us -> 95.7 us (0.938)
  local copies, waits for them, and re-layouts: 9.77 us -> 2.36 us
  Pallas kernels: 90.8 us -> 91.9 us
    unnamed x13 -> x1, local copies, waits for them, and re-layouts: 7.67 us -> 2.36 us
    reshape x3 -> x0, local copies, waits for them, and re-layouts: 2.1 us -> none  [the longest x1 0.7 us: body(): shift_temporal.reshape(1, D)]
    pallas_call x1, Pallas kernels: 90.8 us -> 91.9 us  [mega(): pl.pallas_call(kernel, out_shape=jax.ShapeDtypeStruct((TOKENS, D), f32),...]
where the time goes in v3:
time: 95.7 us; the launch traced here: 94.9 us
  Pallas kernels  91.9 us (96%)
  local copies, waits for them, and re-layouts  2.36 us (2%)
    pallas_call x1, Pallas kernels, mega(): pl.pallas_call(kernel, out_shape=jax.ShapeDtypeStruct((TOKENS, D), f32),...  91.9 us
    unnamed x1, local copies, waits for them, and re-layouts  2.36 us

profile of v3, /device:TPU:1, one launch (start us, length us, event | category | flops | bytes accessed | tf_op | source)
XLA Modules:
  0.0 94.9 jit_solution(7785843770136429750)
XLA Ops:
  0.7 91.9 %stdit.1 = f32[256,1152]{1,0:T(8,128)} custom-call(s32[1]{0:T(128)S(6)} %copy.13.length_ref, bf16[256,1152]{1,0:T(8,128)(2,1)} %bitcast.8, f32[1152]{0:T(1024)} %shift_hbm.1, f32[1152]{0:T(1024)} %scale_hbm.1, f32[1152]{0:T(1024)} %gate_hbm.1, bf16[3,576,1152]{2,1,0:T(8,128)(2,1)} %bitcast.6, bf16[576,1152]{1,0:T(8,128)(2,1)} %wp_hbm.1, ...), custom_call_target="tpu_custom_call" | custom-call | flops 4000000000 | bytes 12000000 | tf_op jit(solution)/shard_map/stdit/pallas_call | solution.py:378
  92.6 2.4 %copy.14 = f32[1,256,1152]{2,1,0:T(8,128)} copy(f32[1,256,1152]{2,1,0:T(8,128)} %bitcast.5) | data formatting | bytes 2359296

commit v4 on v3

v4 whole, which is shorter than its diff:
```python
import jax
import jax.numpy as jnp
from jax import lax
from jax.experimental import pallas as pl
from jax.experimental.pallas import tpu as pltpu
from jax.sharding import PartitionSpec as P

D = 1152
HD = 72
HEADS = 8
WIDTH = HEADS * HD
TOKENS = 256
FRAMES = 128
LOW, HIGH = 640, 512
NZ = 8
NQ = 16
TEXT_LEN = 300
TEXT_ROWS = 304
EXP_SCALE = HD ** (-0.5) * 1.4426950408889634
MESH = pl.DeviceIdType.MESH


def rows_of(index, size):
    return pl.ds(pl.multiple_of(index * size, size), size)


def attend(query, key, value, visible, store):
    tiles = [None] * 5
    for head in range(HEADS):
        low, high = head * HD, (head + 1) * HD
        first, last = low // 128, (high - 1) // 128
        start, end = first * 128, min((last + 1) * 128, WIDTH)
        rows = query[:, start:end]
        lane = lax.broadcasted_iota(jnp.int32, rows.shape, 1) + start
        rows = jnp.where((lane >= low) & (lane < high), rows, jnp.zeros_like(rows))
        scores = lax.dot_general(
            rows, key[:, start:end], (((1,), (1,)), ((), ())), preferred_element_type=jnp.float32
        )
        if visible is not None:
            scores = jnp.where(visible, scores, -1e30)
        top = jnp.max(scores, axis=-1, keepdims=True)
        weights = jnp.exp2((scores - top) * EXP_SCALE)
        total = jnp.sum(weights, axis=-1, keepdims=True)
        mixed = jnp.dot(
            weights.astype(jnp.bfloat16), value[:, start:end], preferred_element_type=jnp.float32
        ) * (1.0 / total)
        for tile in range(first, last + 1):
            piece = mixed[:, tile * 128 - start : min((tile + 1) * 128, WIDTH) - start]
            if tiles[tile] is not None:
                lane = lax.broadcasted_iota(jnp.int32, piece.shape, 1) + tile * 128
                piece = jnp.where(lane >= low, piece, tiles[tile])
            tiles[tile] = piece
            if high >= min((tile + 1) * 128, WIDTH):
                store(tile, piece.astype(jnp.bfloat16))


def across(rows, weights):
    return lax.dot_general(
        rows, weights, (((1,), (1,)), ((), ())), preferred_element_type=jnp.float32
    ).astype(jnp.bfloat16)


def kernel(
    length_ref, x_hbm, shift_hbm, scale_hbm, gate_hbm, wqkv_hbm, wp_hbm, wcq_hbm, wcp_hbm, ckv_hbm, te_hbm,
    out_hbm,
    shift_ref, scale_ref, gate_ref, ckv_ref, te_ref, wqkv, wp, wp_far, wcq, wcp, wcp_far,
    s1, t32, u32, v32, msg, xin, normed, qkv, att, att_far, branch, om, o2, back,
    te_pad, part, core_in, part_x, x_in, part_z, z_in, part_y, y_in, full, tk, tv,
    load_sem, w_send, w_recv, s1_send, s1_recv, s2_send, s2_recv,
    a_send, a_recv, o2_send, o2_recv, o1_send, o1_recv,
    c_send, c_recv, x_send, x_recv, z_send, z_recv, y_send, y_recv, own_sem,
):
    seq, hi = lax.axis_index("seq"), lax.axis_index("tp")
    z, q = seq // NQ, lax.rem(seq, NQ)
    core, spot = lax.rem(q, 2), q // 2

    def other_y(index):
        return index + 2 - 4 * lax.rem(index // 2, 2)

    def group_of(index):
        return index + hi * (other_y(index) - index)

    def place_of(index):
        group = group_of(index)
        return lax.rem(group, 2) * 8 + group // 2

    def at_z(index):
        return (index * NQ + q, hi)

    def at_q(index):
        return (z * NQ + index, hi)

    def at_x(index):
        return at_q(index * 4 + lax.rem(q, 4))

    x = q // 4
    pair = (z * NQ + other_y(q), 1 - hi)
    sibling = at_q(q + 1 - 2 * core)

    loads = [
        pltpu.make_async_copy(source, target, load_sem.at[n])
        for n, (source, target) in enumerate(
            (
                (te_hbm, te_ref), (ckv_hbm, ckv_ref), (shift_hbm, shift_ref), (scale_hbm, scale_ref),
                (gate_hbm, gate_ref), (wqkv_hbm, wqkv), (wp_hbm, wp), (wcq_hbm, wcq), (wcp_hbm, wcp),
            )
        )
    ]
    for load in loads:
        load.start()

    barrier = pltpu.get_barrier_semaphore()
    for step in range(1, NZ):
        pl.semaphore_signal(barrier, inc=1, device_id=at_z(lax.rem(z + step, NZ)), device_id_type=MESH)
    for step in range(1, NQ):
        pl.semaphore_signal(barrier, inc=1, device_id=at_q(lax.rem(q + step, NQ)), device_id_type=MESH)
    pl.semaphore_signal(barrier, inc=1, device_id=pair, device_id_type=MESH)

    def remote(source, target, send, recv, device):
        return pltpu.make_async_remote_copy(
            src_ref=source, dst_ref=target, send_sem=send, recv_sem=recv, device_id=device, device_id_type=MESH
        )

    sent = []

    def send(source, target, send_sem, recv_sem, device, when=None):
        copy = remote(source, target, send_sem, recv_sem, device)
        if when is None:
            copy.start()
        else:
            pl.when(when)(copy.start)
        sent.append((copy, when))

    def arrived(target, recv_sem, device, when=None):
        copy = remote(target, target, c_send.at[0], recv_sem, device)
        if when is None:
            copy.wait_recv()
        else:
            pl.when(when)(copy.wait_recv)

    def drain():
        for copy, when in sent:
            if when is None:
                copy.wait_send()
            else:
                pl.when(when)(copy.wait_send)
        sent.clear()

    def text_products():
        loads[0].wait()
        loads[1].wait()
        te_pad[...] = jnp.zeros_like(te_pad)
        te_pad[:, :TEXT_LEN] = te_ref[...]
        part[190:] = jnp.zeros((2, 16, 128), jnp.bfloat16)
        for which in range(2):
            product = lax.dot_general(
                te_pad[:, :TEXT_ROWS], ckv_ref[which], (((0,), (0,)), ((), ())), preferred_element_type=jnp.float32
            ).astype(jnp.bfloat16)
            product = jnp.concatenate([product, jnp.zeros((TEXT_ROWS, 64), jnp.bfloat16)], axis=1)
            for r in range(TEXT_ROWS // 16):
                for tile in range(5):
                    part[r * 10 + which * 5 + tile] = product[r * 16 : r * 16 + 16, tile * 128 : tile * 128 + 128]

    def text_send():
        send(part.at[pl.ds(96 - 96 * core, 96)], core_in, c_send.at[0], c_recv.at[0], sibling)

    def text_core_sum():
        arrived(core_in, c_recv.at[0], sibling)
        part_x[...] = (part[pl.ds(96 * core, 96)].astype(jnp.float32) + core_in[...].astype(jnp.float32)).astype(jnp.bfloat16)
        for step in range(1, 4):
            target = lax.rem(x + step, 4)
            send(part_x.at[pl.ds(24 * target, 24)], x_in.at[x], x_send.at[0, step], x_recv.at[0, x], at_x(target))

    def text_x_sum():
        total = part_x[pl.ds(24 * x, 24)].astype(jnp.float32)
        for step in range(1, 4):
            source = lax.rem(x + step, 4)
            arrived(x_in.at[source], x_recv.at[0, source], at_x(source))
            total += x_in[source].astype(jnp.float32)
        part_z[...] = total.astype(jnp.bfloat16)
        for step in range(1, NZ):
            target = lax.rem(z + step, NZ)
            send(part_z.at[pl.ds(3 * target, 3)], z_in.at[z], z_send.at[0, step], z_recv.at[0, z], at_z(target))

    def text_z_sum():
        total = part_z[pl.ds(3 * z, 3)].astype(jnp.float32)
        for step in range(1, NZ):
            source = lax.rem(z + step, NZ)
            arrived(z_in.at[source], z_recv.at[0, source], at_z(source))
            total += z_in[source].astype(jnp.float32)
        part_y[...] = total.astype(jnp.bfloat16)
        send(part_y, y_in, y_send.at[0], y_recv.at[0], at_q(other_y(q)))

    def text_y_sum():
        arrived(y_in, y_recv.at[0], at_q(other_y(q)))
        mine = full.at[pl.ds(96 * core + 24 * x + 3 * z, 3)]
        mine[...] = (part_y[...].astype(jnp.float32) + y_in[...].astype(jnp.float32)).astype(jnp.bfloat16)
        for step in range(1, NZ):
            send(mine, mine, z_send.at[1, step], z_recv.at[1, z], at_z(lax.rem(z + step, NZ)))

    def text_z_gather():
        for step in range(1, NZ):
            source = lax.rem(z + step, NZ)
            arrived(full.at[pl.ds(96 * core + 24 * x + 3 * source, 3)], z_recv.at[1, source], at_z(source))
        mine = full.at[pl.ds(96 * core + 24 * x, 24)]
        for step in range(1, 4):
            send(mine, mine, x_send.at[1, step], x_recv.at[1, x], at_x(lax.rem(x + step, 4)))

    def text_x_gather():
        for step in range(1, 4):
            source = lax.rem(x + step, 4)
            arrived(full.at[pl.ds(96 * core + 24 * source, 24)], x_recv.at[1, source], at_x(source))
        mine = full.at[pl.ds(96 * core, 96)]
        send(mine, mine, c_send.at[1], c_recv.at[1], sibling)

    def text_core_gather():
        arrived(full.at[pl.ds(96 - 96 * core, 96)], c_recv.at[1], sibling)
        for which, target in enumerate((tk, tv)):
            for r in range(TEXT_ROWS // 16):
                for tile in range(5):
                    width = min(128, WIDTH - tile * 128)
                    target[r * 16 : r * 16 + 16, tile * 128 : tile * 128 + width] = full[r * 10 + which * 5 + tile][:, :width]

    half_rows = pl.ds(pl.multiple_of(core * 288, 288), 288)
    other_rows = pl.ds(pl.multiple_of(288 - core * 288, 288), 288)
    own = []

    def location_rows(index, stream):
        return pl.ds(pl.multiple_of(index * 32 + stream * 16, 16), 16)

    def in1_send(stream):
        for n, step in enumerate((4, 3, 5, 2, 6, 1, 7)):
            target = lax.rem(z + step, NZ)
            send(
                x_hbm.at[location_rows(target, stream)],
                s1.at[z, stream], s1_send.at[n, stream], s1_recv.at[z, stream], at_z(target),
            )
        copy = pltpu.make_async_copy(x_hbm.at[location_rows(z, stream)], s1.at[z, stream], own_sem.at[stream])
        copy.start()
        own.append(copy)

    def in1_done(stream):
        own[stream].wait()
        for step in range(1, NZ):
            source = lax.rem(z + step, NZ)
            arrived(s1.at[source, stream], s1_recv.at[source, stream], at_z(source))

    def in2_send(stream):
        def spread_in(tile, carry):
            lanes = pl.ds(pl.multiple_of(tile * 128, 128), 128)
            upper = pl.ds(pl.multiple_of(lax.rem(tile + 5, 9) * 128, 128), 128)
            for n in range(NZ):
                t32[n * 16 : (n + 1) * 16] = s1[n, stream, :, lanes].astype(jnp.float32)
                u32[n * 16 : (n + 1) * 16] = s1[n, stream, :, upper].astype(jnp.float32)
            for n in range(NQ):
                both = jnp.concatenate([t32[pl.ds(n, 8, stride=16), :], u32[pl.ds(n, 8, stride=16), :]], axis=0)
                msg[stream, n, :, lanes] = both.astype(jnp.bfloat16)
            return carry

        lax.fori_loop(0, 5, spread_in, 0)
        for step in (8, 4, 12, 10, 6, 14, 2, 9, 5, 13, 11, 7, 15, 3, 1):
            dest = lax.rem(q + step, NQ)
            send(msg.at[stream, place_of(dest)], xin.at[stream, q], s2_send.at[stream, step], s2_recv.at[stream, q], at_q(dest))
        xin[stream, q] = msg[stream, place_of(q)]

    def in2_done(stream):
        for step in range(1, NQ):
            source = lax.rem(q + step, NQ)
            arrived(xin.at[stream, source], s2_recv.at[stream, source], at_q(source))

    def latent_rows(stream, n):
        first, second = xin[stream, 2 * n].astype(jnp.float32), xin[stream, 2 * n + 1].astype(jnp.float32)
        low = jnp.concatenate([first[:8], second[:8]], axis=0)
        high = jnp.concatenate([first[8:, :HIGH], second[8:, :HIGH]], axis=0)
        return jnp.concatenate([low, high], axis=1)

    def temporal_norm(stream):
        def norm_rows(n, carry):
            values = latent_rows(stream, n)
            center = jnp.mean(values, axis=-1, keepdims=True)
            values = values - center
            spread = jnp.mean(jnp.square(values), axis=-1, keepdims=True)
            values = values * lax.rsqrt(spread + 1e-06) * (1.0 + scale_ref[...].reshape(1, D)) + shift_ref[...].reshape(1, D)
            normed[rows_of(n, 16)] = values.astype(jnp.bfloat16)
            return carry

        lax.fori_loop(0, 8, norm_rows, 0, unroll=2)

    def temporal(stream):
        def project(n, carry):
            qkv[n] = across(normed[...], wqkv[n])
            return carry

        lax.fori_loop(0, 3, project, 0)
        attend(qkv.at[0], qkv.at[1], qkv.at[2], None, put(att.at[0, stream]))
        swap(0, stream)

    def put(target):
        def store(tile, piece):
            target[:, tile * 128 : tile * 128 + piece.shape[1]] = piece

        return store

    def swap(kind, stream):
        send(att.at[kind, stream], att_far.at[kind, stream], a_send.at[kind, stream], a_recv.at[kind, stream], pair)

    def swapped(kind, stream):
        arrived(att_far.at[kind, stream], a_recv.at[kind, stream], pair)

    def mix(stream):
        branch[stream] = jnp.dot(att[0, stream], wp[...], preferred_element_type=jnp.float32)
        swapped(0, stream)
        total = branch[stream] + jnp.dot(att_far[0, stream], wp_far[...], preferred_element_type=jnp.float32)
        branch[stream] = total * gate_ref[...].reshape(1, D)

        def mix_rows(n, carry):
            rows = rows_of(n, 16)
            normed[rows] = (latent_rows(stream, n) + branch[stream, rows]).astype(jnp.bfloat16)
            return carry

        lax.fori_loop(0, 8, mix_rows, 0)
        qkv[0] = across(normed[...], wcq[...])

    def cross(stream):
        text = lax.broadcasted_iota(jnp.int32, (1, TEXT_ROWS), 1)
        attend(qkv.at[0], tk, tv, text < length_ref[0], put(att.at[1, stream]))
        swap(1, stream)
        branch[stream] += jnp.dot(att[1, stream], wcp[...], preferred_element_type=jnp.float32)

    def out2_send(stream):
        branch[stream] += jnp.dot(att_far[1, stream], wcp_far[...], preferred_element_type=jnp.float32)

        def fold(n, carry):
            rows = branch[stream, rows_of(n, 8)]
            high = jnp.concatenate([rows[:, LOW:], jnp.zeros((8, LOW - HIGH), jnp.float32)], axis=1)
            om[stream, n] = jnp.concatenate([rows[:, :LOW], high], axis=0).astype(jnp.bfloat16)
            return carry

        lax.fori_loop(0, NQ, fold, 0, unroll=2)
        place = place_of(q)
        for step in (8, 4, 12, 10, 6, 14, 2, 9, 5, 13, 11, 7, 15, 3, 1):
            dest = lax.rem(q + step, NQ)
            send(om.at[stream, dest], o2.at[stream, place], o2_send.at[stream, step], o2_recv.at[stream, place], at_q(dest))
        o2[stream, place] = om[stream, q]

    def out1_send(stream):
        for step in range(1, NQ):
            source = lax.rem(q + step, NQ)
            arrived(o2.at[stream, place_of(source)], o2_recv.at[stream, place_of(source)], at_q(source))

        def spread_out(tile, carry):
            lanes = pl.ds(pl.multiple_of(tile * 128, 128), 128)
            for n in range(NQ):
                v32[n * 16 : (n + 1) * 16] = o2[stream, n, :, lanes].astype(jnp.float32)
            for n in range(NZ):
                back[stream, n, :, lanes] = v32[pl.ds(n, 16, stride=16), :].astype(jnp.bfloat16)

            @pl.when(tile < 4)
            def _():
                upper = pl.ds(pl.multiple_of(tile * 128 + LOW, 128), 128)
                for n in range(NZ):
                    back[stream, n, :, upper] = v32[pl.ds(n + 8, 16, stride=16), :].astype(jnp.bfloat16)

            return carry

        lax.fori_loop(0, 5, spread_out, 0)
        for n, step in enumerate((4, 3, 5, 2, 6, 1, 7)):
            target = lax.rem(z + step, NZ)
            send(
                back.at[stream, target], out_hbm.at[location_rows(z, stream)],
                o1_send.at[n, stream], o1_recv.at[z, stream], at_z(target),
            )
        copy = pltpu.make_async_copy(back.at[stream, z], out_hbm.at[location_rows(z, stream)], own_sem.at[2 + stream])
        copy.start()
        own.append(copy)

    def out1_done(stream):
        own[2 + stream].wait()
        for step in range(1, NZ):
            source = lax.rem(z + step, NZ)
            arrived(out_hbm.at[location_rows(source, stream)], o1_recv.at[source, stream], at_z(source))

    def far_weights(n, source, target):
        send(source.at[half_rows], target.at[half_rows], w_send.at[n], w_recv.at[n], pair)

    def forward_weights(n, target):
        arrived(target.at[half_rows], w_recv.at[n], pair)
        send(target.at[half_rows], target.at[half_rows], w_send.at[2 + n], w_recv.at[2 + n], sibling)

    text_products()
    pl.semaphore_wait(barrier, NZ - 1 + NQ - 1 + 1)
    in1_send(0)
    far_weights(0, wp_hbm, wp_far)
    in1_send(1)
    text_send()
    far_weights(1, wcp_hbm, wcp_far)
    in1_done(0)
    in2_send(0)
    text_core_sum()
    in1_done(1)
    in2_send(1)
    text_x_sum()
    for n in (2, 3, 4):
        loads[n].wait()
    in2_done(0)
    temporal_norm(0)
    text_z_sum()
    loads[5].wait()
    temporal(0)
    forward_weights(0, wp_far)
    text_y_sum()
    in2_done(1)
    temporal_norm(1)
    text_z_gather()
    temporal(1)
    text_x_gather()
    loads[6].wait()
    loads[7].wait()
    arrived(wp_far.at[other_rows], w_recv.at[2], sibling)
    mix(0)
    text_core_gather()
    loads[8].wait()
    cross(0)
    forward_weights(1, wcp_far)
    mix(1)
    cross(1)
    arrived(wcp_far.at[other_rows], w_recv.at[3], sibling)
    swapped(1, 0)
    out2_send(0)
    swapped(1, 1)
    out2_send(1)
    out1_send(0)
    out1_send(1)
    out1_done(0)
    out1_done(1)
    drain()


def mega(length, x, shift, scale, gate, wqkv, wp, wcq, wcp, ckv, te):
    bf16, f32 = jnp.bfloat16, jnp.float32
    dma, vmem = pltpu.SemaphoreType.DMA, pltpu.VMEM
    return pl.pallas_call(
        kernel,
        out_shape=jax.ShapeDtypeStruct((TOKENS, D), bf16),
        in_specs=[pl.BlockSpec(memory_space=pltpu.SMEM)] + [pl.BlockSpec(memory_space=pltpu.HBM)] * 10,
        out_specs=pl.BlockSpec(memory_space=pltpu.HBM),
        scratch_shapes=[
            vmem((D,), f32), vmem((D,), f32), vmem((D,), f32),
            vmem((2, 32, WIDTH), bf16), vmem((32, TEXT_LEN), bf16),
            vmem((3, WIDTH, D), bf16), vmem((WIDTH, D), bf16), vmem((WIDTH, D), bf16),
            vmem((WIDTH, D), bf16), vmem((WIDTH, D), bf16), vmem((WIDTH, D), bf16),
            vmem((NZ, 2, 16, D), bf16), vmem((128, 128), f32), vmem((128, 128), f32), vmem((256, 128), f32),
            vmem((2, NQ, 16, LOW), bf16), vmem((2, NQ, 16, LOW), bf16),
            vmem((FRAMES, D), bf16), vmem((3, FRAMES, WIDTH), bf16),
            vmem((2, 2, FRAMES, WIDTH), bf16), vmem((2, 2, FRAMES, WIDTH), bf16), vmem((2, FRAMES, D), f32),
            vmem((2, NQ, 16, LOW), bf16), vmem((2, NQ, 16, LOW), bf16), vmem((2, NZ, 16, D), bf16),
            vmem((32, 384), bf16), vmem((192, 16, 128), bf16), vmem((96, 16, 128), bf16), vmem((96, 16, 128), bf16),
            vmem((4, 24, 16, 128), bf16), vmem((24, 16, 128), bf16), vmem((8, 3, 16, 128), bf16),
            vmem((3, 16, 128), bf16), vmem((3, 16, 128), bf16), vmem((192, 16, 128), bf16),
            vmem((TEXT_ROWS, WIDTH), bf16), vmem((TEXT_ROWS, WIDTH), bf16),
            dma((9,)), dma((4,)), dma((4,)), dma((7, 2)), dma((8, 2)), dma((2, 16)), dma((2, 16)),
            dma((2, 2)), dma((2, 2)), dma((2, 16)), dma((2, 16)), dma((7, 2)), dma((8, 2)),
            dma((2,)), dma((2,)), dma((2, 4)), dma((2, 4)), dma((2, 8)), dma((2, 8)), dma((1,)), dma((1,)), dma((4,)),
        ],
        compiler_params=pltpu.CompilerParams(
            collective_id=0, has_side_effects=True, vmem_limit_bytes=60 * 1024 * 1024
        ),
        cost_estimate=pl.CostEstimate(flops=4_000_000_000, bytes_accessed=12_000_000, transcendentals=2_000_000),
        name="stdit",
    )(length, x, shift, scale, gate, wqkv, wp, wcq, wcp, ckv, te)


def body(
    video_latent, shift_temporal, scale_temporal, gate_temporal, temporal_qkv, temporal_proj,
    cross_query, cross_kv, cross_proj, text_embed, text_length,
):
    out = mega(
        text_length, video_latent.reshape(TOKENS, D),
        shift_temporal, scale_temporal, gate_temporal,
        jnp.transpose(temporal_qkv, (1, 2, 0)), temporal_proj, cross_query.T, cross_proj, cross_kv, text_embed.T,
    )
    return video_latent.astype(jnp.float32) + out.reshape(1, TOKENS, D).astype(jnp.float32)


def solution(mesh):
    return jax.shard_map(
        body,
        mesh=mesh,
        in_specs=(
            P("seq", None, None), P(), P(), P(), P(None, None, "tp"), P("tp", None), P(None, "tp"),
            P(None, "seq", "tp"), P("tp", None), P(None, "seq"), P(),
        ),
        out_specs=P("seq", None, None),
        check_vma=False,
    )
```

time: 95.7 us -> 87 us (0.909)
  Pallas kernels: 91.9 us -> 83.9 us
  local copies, waits for them, and re-layouts: 2.36 us -> 0.01 us
  other arithmetic: 0 us -> 2.19 us
    pallas_call x1, Pallas kernels: 91.9 us -> 83.9 us  [mega(): pl.pallas_call(kernel, out_shape=jax.ShapeDtypeStruct((TOKENS, D), bf16),...]
    unnamed x1 -> x2, local copies, waits for them, and re-layouts: 2.36 us -> 0.01 us
    add x0 -> x1, other arithmetic: none -> 2.19 us  [body(): video_latent.astype(jnp.float32)]
where the time goes in v4:
time: 87 us; the launch traced here: 86.8 us
  Pallas kernels  83.9 us (96%)
  other arithmetic  2.19 us (3%)
    pallas_call x1, Pallas kernels, mega(): pl.pallas_call(kernel, out_shape=jax.ShapeDtypeStruct((TOKENS, D), bf16),...  83.9 us
    add x1, other arithmetic, body(): video_latent.astype(jnp.float32)  2.19 us

profile of v4, /device:TPU:1, one launch (start us, length us, event | category | flops | bytes accessed | tf_op | source)
XLA Modules:
  0.0 86.8 jit_solution(7168317341077111284)
XLA Ops:
  0.7 0.0 copy-start
  0.7 83.9 %stdit.1 = bf16[256,1152]{1,0:T(8,128)(2,1)} custom-call(s32[1]{0:T(128)S(6)} %copy.12.length_ref, bf16[256,1152]{1,0:T(8,128)(2,1)} %bitcast.7, f32[1152]{0:T(1024)} %shift_hbm.1, f32[1152]{0:T(1024)} %scale_hbm.1, f32[1152]{0:T(1024)} %gate_hbm.1, bf16[3,576,1152]{2,1,0:T(8,128)(2,1)} %bitcast.8, bf16[576,1152]{1,0:T(8,128)(2,1)} %wp_hbm.1, ...), custom_call_target="tpu_custom_call" | custom-call | flops 4000000000 | bytes 12000000 | tf_op jit(solution)/shard_map/stdit/pallas_call | solution.py:442
  84.6 0.0 copy-done
  84.6 2.2 %convert_add_fusion = f32[1,256,1152]{2,1,0:T(8,128)} fusion(bf16[1,256,1152]{2,1,0:T(8,128)(2,1)S(1)} %copy-done, bf16[256,1152]{1,0:T(8,128)(2,1)} %stdit.1), kind=kLoop, calls=%fused_computation | loop fusion | flops 884736 | bytes 2359296 | tf_op jit(solution)/shard_map/add | solution.py:482
Async XLA Ops:
  0.7 83.9 %copy-start = (bf16[1,256,1152]{2,1,0:T(8,128)(2,1)S(1)}, bf16[1,256,1152]{2,1,0:T(8,128)(2,1)}, u32[]{:S(2)}) copy-start(bf16[1,256,1152]{2,1,0:T(8,128)(2,1)} %param.11) | copy-start | bytes 1769476

commit v5 on v4

--- a/solution.py
+++ b/solution.py
@@ -24,47 +24,31 @@
     return pl.ds(pl.multiple_of(index * size, size), size)
 
 
-def attend(query, key, value, visible, store):
-    tiles = [None] * 5
-    for head in range(HEADS):
-        low, high = head * HD, (head + 1) * HD
-        first, last = low // 128, (high - 1) // 128
-        start, end = first * 128, min((last + 1) * 128, WIDTH)
-        rows = query[:, start:end]
-        lane = lax.broadcasted_iota(jnp.int32, rows.shape, 1) + start
-        rows = jnp.where((lane >= low) & (lane < high), rows, jnp.zeros_like(rows))
-        scores = lax.dot_general(
-            rows, key[:, start:end], (((1,), (1,)), ((), ())), preferred_element_type=jnp.float32
-        )
-        if visible is not None:
-            scores = jnp.where(visible, scores, -1e30)
-        top = jnp.max(scores, axis=-1, keepdims=True)
-        weights = jnp.exp2((scores - top) * EXP_SCALE)
-        total = jnp.sum(weights, axis=-1, keepdims=True)
-        mixed = jnp.dot(
-            weights.astype(jnp.bfloat16), value[:, start:end], preferred_element_type=jnp.float32
-        ) * (1.0 / total)
-        for tile in range(first, last + 1):
-            piece = mixed[:, tile * 128 - start : min((tile + 1) * 128, WIDTH) - start]
-            if tiles[tile] is not None:
-                lane = lax.broadcasted_iota(jnp.int32, piece.shape, 1) + tile * 128
-                piece = jnp.where(lane >= low, piece, tiles[tile])
-            tiles[tile] = piece
-            if high >= min((tile + 1) * 128, WIDTH):
-                store(tile, piece.astype(jnp.bfloat16))
-
-
-def across(rows, weights):
-    return lax.dot_general(
-        rows, weights, (((1,), (1,)), ((), ())), preferred_element_type=jnp.float32
-    ).astype(jnp.bfloat16)
+def dot(a, b, dims):
+    return lax.dot_general(a, b, (dims, ((), ())), preferred_element_type=jnp.float32)
+
+
+def attend(scores_of, value_of, visible, target):
+    for group in range(0, HEADS, 4):
+        scores = [scores_of(head) for head in range(group, group + 4)]
+        weights, totals = [], []
+        for score in scores:
+            if visible is not None:
+                score = jnp.where(visible, score, -1e30)
+            top = jnp.max(score, axis=0, keepdims=True)
+            weight = jnp.exp2((score - top) * EXP_SCALE)
+            totals.append(1.0 / jnp.sum(weight, axis=0, keepdims=True))
+            weights.append(weight.astype(jnp.bfloat16))
+        mixed = [dot(value_of(group + n), weights[n], ((1,), (0,))) * totals[n] for n in range(4)]
+        for n in (0, 2):
+            target[(group + n) * HD : (group + n + 2) * HD] = jnp.concatenate(mixed[n : n + 2], axis=0).astype(jnp.bfloat16)
 
 
 def kernel(
     length_ref, x_hbm, shift_hbm, scale_hbm, gate_hbm, wqkv_hbm, wp_hbm, wcq_hbm, wcp_hbm, ckv_hbm, te_hbm,
     out_hbm,
-    shift_ref, scale_ref, gate_ref, ckv_ref, te_ref, wqkv, wp, wp_far, wcq, wcp, wcp_far,
-    s1, t32, u32, v32, msg, xin, normed, qkv, att, att_far, branch, om, o2, back,
+    shift_ref, scale_ref, gate_ref, ckv_ref, te_ref, wqkv, wp, wp_far, wcq, wcp,
+    s1, t32, u32, v32, msg, xin, normed, qkv, att, att_far, branch, partial, give, taken, om, o2, back,
     te_pad, part, core_in, part_x, x_in, part_z, z_in, part_y, y_in, full, tk, tv,
     load_sem, w_send, w_recv, s1_send, s1_recv, s2_send, s2_recv,
     a_send, a_recv, o2_send, o2_recv, o1_send, o1_recv,
@@ -215,11 +199,14 @@
 
     def text_core_gather():
         arrived(full.at[pl.ds(96 - 96 * core, 96)], c_recv.at[1], sibling)
-        for which, target in enumerate((tk, tv)):
+        for tile in range(5):
+            width = min(128, WIDTH - tile * 128)
+            rows = []
             for r in range(TEXT_ROWS // 16):
-                for tile in range(5):
-                    width = min(128, WIDTH - tile * 128)
-                    target[r * 16 : r * 16 + 16, tile * 128 : tile * 128 + width] = full[r * 10 + which * 5 + tile][:, :width]
+                tk[r * 16 : r * 16 + 16, tile * 128 : tile * 128 + width] = full[r * 10 + tile][:, :width]
+                rows.append(full[r * 10 + 5 + tile].astype(jnp.float32))
+            rows.append(jnp.zeros((384 - TEXT_ROWS, 128), jnp.float32))
+            tv[tile * 128 : (tile + 1) * 128] = jnp.concatenate(rows, axis=0).T
 
     half_rows = pl.ds(pl.multiple_of(core * 288, 288), 288)
     other_rows = pl.ds(pl.multiple_of(288 - core * 288, 288), 288)
@@ -286,31 +273,25 @@
 
         lax.fori_loop(0, 8, norm_rows, 0, unroll=2)
 
+    def head_rows(which, head):
+        return qkv[which, head * HD : (head + 1) * HD].astype(jnp.bfloat16)
+
     def temporal(stream):
         def project(n, carry):
-            qkv[n] = across(normed[...], wqkv[n])
+            qkv[n] = dot(wqkv[n], normed[...], ((1,), (1,)))
             return carry
 
         lax.fori_loop(0, 3, project, 0)
-        attend(qkv.at[0], qkv.at[1], qkv.at[2], None, put(att.at[0, stream]))
-        swap(0, stream)
-
-    def put(target):
-        def store(tile, piece):
-            target[:, tile * 128 : tile * 128 + piece.shape[1]] = piece
-
-        return store
-
-    def swap(kind, stream):
-        send(att.at[kind, stream], att_far.at[kind, stream], a_send.at[kind, stream], a_recv.at[kind, stream], pair)
-
-    def swapped(kind, stream):
-        arrived(att_far.at[kind, stream], a_recv.at[kind, stream], pair)
+        attend(
+            lambda head: dot(head_rows(1, head), head_rows(0, head), ((0,), (0,))),
+            lambda head: head_rows(2, head), None, att.at[0, stream],
+        )
+        send(att.at[0, stream], att_far.at[stream], a_send.at[0, stream], a_recv.at[0, stream], pair)
 
     def mix(stream):
-        branch[stream] = jnp.dot(att[0, stream], wp[...], preferred_element_type=jnp.float32)
-        swapped(0, stream)
-        total = branch[stream] + jnp.dot(att_far[0, stream], wp_far[...], preferred_element_type=jnp.float32)
+        branch[stream] = dot(att[0, stream], wp[...], ((0,), (0,)))
+        arrived(att_far.at[stream], a_recv.at[0, stream], pair)
+        total = branch[stream] + dot(att_far[stream], wp_far[...], ((0,), (0,)))
         branch[stream] = total * gate_ref[...].reshape(1, D)
 
         def mix_rows(n, carry):
@@ -318,36 +299,59 @@
             normed[rows] = (latent_rows(stream, n) + branch[stream, rows]).astype(jnp.bfloat16)
             return carry
 
-        lax.fori_loop(0, 8, mix_rows, 0)
-        qkv[0] = across(normed[...], wcq[...])
+        lax.fori_loop(0, 8, mix_rows, 0, unroll=2)
+        qkv[0] = dot(wcq[...], normed[...], ((1,), (1,)))
 
     def cross(stream):
-        text = lax.broadcasted_iota(jnp.int32, (1, TEXT_ROWS), 1)
-        attend(qkv.at[0], tk, tv, text < length_ref[0], put(att.at[1, stream]))
-        swap(1, stream)
-        branch[stream] += jnp.dot(att[1, stream], wcp[...], preferred_element_type=jnp.float32)
+        row = lax.broadcasted_iota(jnp.int32, (TEXT_ROWS, FRAMES), 0)
+
+        def scores_of(head):
+            low, high = head * HD, (head + 1) * HD
+            start, end = low // 128 * 128, min(-(-high // 128) * 128, WIDTH)
+            place = lax.broadcasted_iota(jnp.int32, (end - start, FRAMES), 0) + start
+            query = jnp.where((place >= low) & (place < high), qkv[0, start:end], 0.0).astype(jnp.bfloat16)
+            return dot(tk[:, start:end], query, ((1,), (0,)))
+
+        def value_of(head):
+            return tv[head * HD : (head + 1) * HD, :TEXT_ROWS].astype(jnp.bfloat16)
+
+        attend(scores_of, value_of, row < length_ref[0], att.at[1, stream])
+        partial[...] = dot(att[1, stream], wcp[...], ((0,), (0,)))
+
+        def fold_partial(n, carry):
+            give[stream, n] = fold(partial[rows_of(n, 8)]).astype(jnp.bfloat16)
+            return carry
+
+        lax.fori_loop(0, NQ, fold_partial, 0, unroll=2)
+        send(give.at[stream], taken.at[stream], a_send.at[1, stream], a_recv.at[1, stream], pair)
+
+    def fold(rows):
+        high = jnp.concatenate([rows[:, LOW:], jnp.zeros((8, LOW - HIGH), jnp.float32)], axis=1)
+        return jnp.concatenate([rows[:, :LOW], high], axis=0)
+
+    def out2_add(stream):
+        arrived(taken.at[stream], a_recv.at[1, stream], pair)
+
+        def add_rows(n, carry):
+            both = give[stream, n].astype(jnp.float32) + taken[stream, n].astype(jnp.float32)
+            om[stream, n] = (fold(branch[stream, rows_of(n, 8)]) + both).astype(jnp.bfloat16)
+            return carry
+
+        lax.fori_loop(0, NQ, add_rows, 0, unroll=2)
 
     def out2_send(stream):
-        branch[stream] += jnp.dot(att_far[1, stream], wcp_far[...], preferred_element_type=jnp.float32)
-
-        def fold(n, carry):
-            rows = branch[stream, rows_of(n, 8)]
-            high = jnp.concatenate([rows[:, LOW:], jnp.zeros((8, LOW - HIGH), jnp.float32)], axis=1)
-            om[stream, n] = jnp.concatenate([rows[:, :LOW], high], axis=0).astype(jnp.bfloat16)
-            return carry
-
-        lax.fori_loop(0, NQ, fold, 0, unroll=2)
         place = place_of(q)
         for step in (8, 4, 12, 10, 6, 14, 2, 9, 5, 13, 11, 7, 15, 3, 1):
             dest = lax.rem(q + step, NQ)
             send(om.at[stream, dest], o2.at[stream, place], o2_send.at[stream, step], o2_recv.at[stream, place], at_q(dest))
         o2[stream, place] = om[stream, q]
 
-    def out1_send(stream):
+    def out2_done(stream):
         for step in range(1, NQ):
             source = lax.rem(q + step, NQ)
             arrived(o2.at[stream, place_of(source)], o2_recv.at[stream, place_of(source)], at_q(source))
 
+    def out1_send(stream):
         def spread_out(tile, carry):
             lanes = pl.ds(pl.multiple_of(tile * 128, 128), 128)
             for n in range(NQ):
@@ -380,56 +384,49 @@
             source = lax.rem(z + step, NZ)
             arrived(out_hbm.at[location_rows(source, stream)], o1_recv.at[source, stream], at_z(source))
 
-    def far_weights(n, source, target):
-        send(source.at[half_rows], target.at[half_rows], w_send.at[n], w_recv.at[n], pair)
-
-    def forward_weights(n, target):
-        arrived(target.at[half_rows], w_recv.at[n], pair)
-        send(target.at[half_rows], target.at[half_rows], w_send.at[2 + n], w_recv.at[2 + n], sibling)
-
     text_products()
     pl.semaphore_wait(barrier, NZ - 1 + NQ - 1 + 1)
     in1_send(0)
-    far_weights(0, wp_hbm, wp_far)
+    text_send()
+    send(wp_hbm.at[half_rows], wp_far.at[half_rows], w_send.at[0], w_recv.at[0], pair)
     in1_send(1)
-    text_send()
-    far_weights(1, wcp_hbm, wcp_far)
+    text_core_sum()
+    text_x_sum()
     in1_done(0)
     in2_send(0)
-    text_core_sum()
     in1_done(1)
     in2_send(1)
-    text_x_sum()
+    text_z_sum()
     for n in (2, 3, 4):
         loads[n].wait()
     in2_done(0)
     temporal_norm(0)
-    text_z_sum()
     loads[5].wait()
+    text_y_sum()
     temporal(0)
-    forward_weights(0, wp_far)
-    text_y_sum()
+    arrived(wp_far.at[half_rows], w_recv.at[0], pair)
+    send(wp_far.at[half_rows], wp_far.at[half_rows], w_send.at[1], w_recv.at[1], sibling)
+    text_z_gather()
     in2_done(1)
     temporal_norm(1)
-    text_z_gather()
+    text_x_gather()
     temporal(1)
-    text_x_gather()
     loads[6].wait()
     loads[7].wait()
-    arrived(wp_far.at[other_rows], w_recv.at[2], sibling)
+    arrived(wp_far.at[other_rows], w_recv.at[1], sibling)
+    text_core_gather()
     mix(0)
-    text_core_gather()
     loads[8].wait()
     cross(0)
-    forward_weights(1, wcp_far)
     mix(1)
     cross(1)
-    arrived(wcp_far.at[other_rows], w_recv.at[3], sibling)
-    swapped(1, 0)
+    out2_add(0)
     out2_send(0)
-    swapped(1, 1)
+    out2_add(1)
     out2_send(1)
+    out2_done(0)
     out1_send(0)
+    out2_done(1)
     out1_send(1)
     out1_done(0)
     out1_done(1)
@@ -448,17 +445,19 @@
             vmem((D,), f32), vmem((D,), f32), vmem((D,), f32),
             vmem((2, 32, WIDTH), bf16), vmem((32, TEXT_LEN), bf16),
             vmem((3, WIDTH, D), bf16), vmem((WIDTH, D), bf16), vmem((WIDTH, D), bf16),
-            vmem((WIDTH, D), bf16), vmem((WIDTH, D), bf16), vmem((WIDTH, D), bf16),
+            vmem((WIDTH, D), bf16), vmem((WIDTH, D), bf16),
             vmem((NZ, 2, 16, D), bf16), vmem((128, 128), f32), vmem((128, 128), f32), vmem((256, 128), f32),
             vmem((2, NQ, 16, LOW), bf16), vmem((2, NQ, 16, LOW), bf16),
-            vmem((FRAMES, D), bf16), vmem((3, FRAMES, WIDTH), bf16),
-            vmem((2, 2, FRAMES, WIDTH), bf16), vmem((2, 2, FRAMES, WIDTH), bf16), vmem((2, FRAMES, D), f32),
+            vmem((FRAMES, D), bf16), vmem((3, WIDTH, FRAMES), f32),
+            vmem((2, 2, WIDTH, FRAMES), bf16), vmem((2, WIDTH, FRAMES), bf16),
+            vmem((2, FRAMES, D), f32), vmem((FRAMES, D), f32),
+            vmem((2, NQ, 16, LOW), bf16), vmem((2, NQ, 16, LOW), bf16),
             vmem((2, NQ, 16, LOW), bf16), vmem((2, NQ, 16, LOW), bf16), vmem((2, NZ, 16, D), bf16),
             vmem((32, 384), bf16), vmem((192, 16, 128), bf16), vmem((96, 16, 128), bf16), vmem((96, 16, 128), bf16),
             vmem((4, 24, 16, 128), bf16), vmem((24, 16, 128), bf16), vmem((8, 3, 16, 128), bf16),
             vmem((3, 16, 128), bf16), vmem((3, 16, 128), bf16), vmem((192, 16, 128), bf16),
-            vmem((TEXT_ROWS, WIDTH), bf16), vmem((TEXT_ROWS, WIDTH), bf16),
-            dma((9,)), dma((4,)), dma((4,)), dma((7, 2)), dma((8, 2)), dma((2, 16)), dma((2, 16)),
+            vmem((TEXT_ROWS, WIDTH), bf16), vmem((640, 384), f32),
+            dma((9,)), dma((2,)), dma((2,)), dma((7, 2)), dma((8, 2)), dma((2, 16)), dma((2, 16)),
             dma((2, 2)), dma((2, 2)), dma((2, 16)), dma((2, 16)), dma((7, 2)), dma((8, 2)),
             dma((2,)), dma((2,)), dma((2, 4)), dma((2, 4)), dma((2, 8)), dma((2, 8)), dma((1,)), dma((1,)), dma((4,)),
         ],

time: 87 us -> 83.3 us (0.957)
  Pallas kernels: 83.9 us -> 80.3 us
    pallas_call x1, Pallas kernels: 83.9 us -> 80.3 us  [mega(): pl.pallas_call(kernel, out_shape=jax.ShapeDtypeStruct((TOKENS, D), bf16),...]
where the time goes in v5:
time: 83.3 us; the launch traced here: 83.2 us
  Pallas kernels  80.3 us (96%)
  other arithmetic  2.19 us (3%)
    pallas_call x1, Pallas kernels, mega(): pl.pallas_call(kernel, out_shape=jax.ShapeDtypeStruct((TOKENS, D), bf16),...  80.3 us
    add x1, other arithmetic, body(): video_latent.astype(jnp.float32)  2.19 us

profile of v5, /device:TPU:1, one launch (start us, length us, event | category | flops | bytes accessed | tf_op | source)
XLA Modules:
  0.0 83.2 jit_solution(159396792102413894)
XLA Ops:
  0.7 0.0 copy-start
  0.7 80.3 %stdit.1 = bf16[256,1152]{1,0:T(8,128)(2,1)} custom-call(s32[1]{0:T(128)S(6)} %copy.12.length_ref, bf16[256,1152]{1,0:T(8,128)(2,1)} %bitcast.7, f32[1152]{0:T(1024)} %shift_hbm.1, f32[1152]{0:T(1024)} %scale_hbm.1, f32[1152]{0:T(1024)} %gate_hbm.1, bf16[3,576,1152]{2,1,0:T(8,128)(2,1)} %bitcast.8, bf16[576,1152]{1,0:T(8,128)(2,1)} %wp_hbm.1, ...), custom_call_target="tpu_custom_call" | custom-call | flops 4000000000 | bytes 12000000 | tf_op jit(solution)/shard_map/stdit/pallas_call | solution.py:439
  81.0 0.0 copy-done
  81.0 2.2 %convert_add_fusion = f32[1,256,1152]{2,1,0:T(8,128)} fusion(bf16[1,256,1152]{2,1,0:T(8,128)(2,1)S(1)} %copy-done, bf16[256,1152]{1,0:T(8,128)(2,1)} %stdit.1), kind=kLoop, calls=%fused_computation | loop fusion | flops 884736 | bytes 2359296 | tf_op jit(solution)/shard_map/add | solution.py:481
Async XLA Ops:
  0.7 80.3 %copy-start = (bf16[1,256,1152]{2,1,0:T(8,128)(2,1)S(1)}, bf16[1,256,1152]{2,1,0:T(8,128)(2,1)}, u32[]{:S(2)}) copy-start(bf16[1,256,1152]{2,1,0:T(8,128)(2,1)} %param.11) | copy-start | bytes 1769476

commit v6 on v5

--- a/solution.py
+++ b/solution.py
@@ -47,12 +47,12 @@
 def kernel(
     length_ref, x_hbm, shift_hbm, scale_hbm, gate_hbm, wqkv_hbm, wp_hbm, wcq_hbm, wcp_hbm, ckv_hbm, te_hbm,
     out_hbm,
-    shift_ref, scale_ref, gate_ref, ckv_ref, te_ref, wqkv, wp, wp_far, wcq, wcp,
-    s1, t32, u32, v32, msg, xin, normed, qkv, att, att_far, branch, partial, give, taken, om, o2, back,
-    te_pad, part, core_in, part_x, x_in, part_z, z_in, part_y, y_in, full, tk, tv,
+    shift_ref, scale_ref, gate_ref, ckv_ref, te_ref, wqkv, wp, wp_far, wcq, wcp, wcp_far,
+    s1, t32, u32, v32, msg, xin, normed, qkv, asked, att, att_far, branch, partial, om, o2, back,
+    te_pad, part, core_in, part_x, x_in, part_z, z_in, z_full, full, tk, tv,
     load_sem, w_send, w_recv, s1_send, s1_recv, s2_send, s2_recv,
     a_send, a_recv, o2_send, o2_recv, o1_send, o1_recv,
-    c_send, c_recv, x_send, x_recv, z_send, z_recv, y_send, y_recv, own_sem,
+    c_send, c_recv, x_send, x_recv, z_send, z_recv, own_sem,
 ):
     seq, hi = lax.axis_index("seq"), lax.axis_index("tp")
     z, q = seq // NQ, lax.rem(seq, NQ)
@@ -74,10 +74,9 @@
     def at_q(index):
         return (z * NQ + index, hi)
 
-    def at_x(index):
-        return at_q(index * 4 + lax.rem(q, 4))
-
-    x = q // 4
+    def at_spot(index):
+        return at_q(2 * index + core)
+
     pair = (z * NQ + other_y(q), 1 - hi)
     sibling = at_q(q + 1 - 2 * core)
 
@@ -151,49 +150,45 @@
     def text_core_sum():
         arrived(core_in, c_recv.at[0], sibling)
         part_x[...] = (part[pl.ds(96 * core, 96)].astype(jnp.float32) + core_in[...].astype(jnp.float32)).astype(jnp.bfloat16)
-        for step in range(1, 4):
-            target = lax.rem(x + step, 4)
-            send(part_x.at[pl.ds(24 * target, 24)], x_in.at[x], x_send.at[0, step], x_recv.at[0, x], at_x(target))
+        for step in (4, 6, 2, 5, 3, 7, 1):
+            target = lax.rem(spot + step, 8)
+            send(part_x.at[pl.ds(12 * target, 12)], x_in.at[spot], x_send.at[0, step], x_recv.at[0, spot], at_spot(target))
 
     def text_x_sum():
-        total = part_x[pl.ds(24 * x, 24)].astype(jnp.float32)
-        for step in range(1, 4):
-            source = lax.rem(x + step, 4)
-            arrived(x_in.at[source], x_recv.at[0, source], at_x(source))
+        total = part_x[pl.ds(12 * spot, 12)].astype(jnp.float32)
+        for step in range(1, 8):
+            source = lax.rem(spot + step, 8)
+            arrived(x_in.at[source], x_recv.at[0, source], at_spot(source))
             total += x_in[source].astype(jnp.float32)
-        part_z[...] = total.astype(jnp.bfloat16)
-        for step in range(1, NZ):
+        part_z[...] = total.reshape(24, 8, 128)
+        for step in (4, 3, 5, 2, 6, 1, 7):
             target = lax.rem(z + step, NZ)
             send(part_z.at[pl.ds(3 * target, 3)], z_in.at[z], z_send.at[0, step], z_recv.at[0, z], at_z(target))
 
     def text_z_sum():
-        total = part_z[pl.ds(3 * z, 3)].astype(jnp.float32)
+        total = part_z[pl.ds(3 * z, 3)]
         for step in range(1, NZ):
             source = lax.rem(z + step, NZ)
             arrived(z_in.at[source], z_recv.at[0, source], at_z(source))
-            total += z_in[source].astype(jnp.float32)
-        part_y[...] = total.astype(jnp.bfloat16)
-        send(part_y, y_in, y_send.at[0], y_recv.at[0], at_q(other_y(q)))
-
-    def text_y_sum():
-        arrived(y_in, y_recv.at[0], at_q(other_y(q)))
-        mine = full.at[pl.ds(96 * core + 24 * x + 3 * z, 3)]
-        mine[...] = (part_y[...].astype(jnp.float32) + y_in[...].astype(jnp.float32)).astype(jnp.bfloat16)
-        for step in range(1, NZ):
+            total += z_in[source]
+        mine = z_full.at[pl.ds(3 * z, 3)]
+        mine[...] = total
+        for step in (4, 3, 5, 2, 6, 1, 7):
             send(mine, mine, z_send.at[1, step], z_recv.at[1, z], at_z(lax.rem(z + step, NZ)))
 
     def text_z_gather():
         for step in range(1, NZ):
             source = lax.rem(z + step, NZ)
-            arrived(full.at[pl.ds(96 * core + 24 * x + 3 * source, 3)], z_recv.at[1, source], at_z(source))
-        mine = full.at[pl.ds(96 * core + 24 * x, 24)]
-        for step in range(1, 4):
-            send(mine, mine, x_send.at[1, step], x_recv.at[1, x], at_x(lax.rem(x + step, 4)))
+            arrived(z_full.at[pl.ds(3 * source, 3)], z_recv.at[1, source], at_z(source))
+        mine = full.at[pl.ds(96 * core + 12 * spot, 12)]
+        mine[...] = z_full[...].reshape(12, 16, 128).astype(jnp.bfloat16)
+        for step in (4, 6, 2, 5, 3, 7, 1):
+            send(mine, mine, x_send.at[1, step], x_recv.at[1, spot], at_spot(lax.rem(spot + step, 8)))
 
     def text_x_gather():
-        for step in range(1, 4):
-            source = lax.rem(x + step, 4)
-            arrived(full.at[pl.ds(96 * core + 24 * source, 24)], x_recv.at[1, source], at_x(source))
+        for step in range(1, 8):
+            source = lax.rem(spot + step, 8)
+            arrived(full.at[pl.ds(96 * core + 12 * source, 12)], x_recv.at[1, source], at_spot(source))
         mine = full.at[pl.ds(96 * core, 96)]
         send(mine, mine, c_send.at[1], c_recv.at[1], sibling)
 
@@ -209,6 +204,10 @@
             tv[tile * 128 : (tile + 1) * 128] = jnp.concatenate(rows, axis=0).T
 
     half_rows = pl.ds(pl.multiple_of(core * 288, 288), 288)
+    odd_x = lax.rem(q // 4, 2)
+    beside = at_q(q + 4 - 8 * odd_x)
+    quarter_rows = pl.ds(pl.multiple_of(core * 288 + odd_x * 144, 16), 144)
+    beside_rows = pl.ds(pl.multiple_of(core * 288 + 144 - odd_x * 144, 16), 144)
     other_rows = pl.ds(pl.multiple_of(288 - core * 288, 288), 288)
     own = []
 
@@ -286,12 +285,12 @@
             lambda head: dot(head_rows(1, head), head_rows(0, head), ((0,), (0,))),
             lambda head: head_rows(2, head), None, att.at[0, stream],
         )
-        send(att.at[0, stream], att_far.at[stream], a_send.at[0, stream], a_recv.at[0, stream], pair)
+        send(att.at[0, stream], att_far.at[0, stream], a_send.at[0, stream], a_recv.at[0, stream], pair)
 
     def mix(stream):
         branch[stream] = dot(att[0, stream], wp[...], ((0,), (0,)))
-        arrived(att_far.at[stream], a_recv.at[0, stream], pair)
-        total = branch[stream] + dot(att_far[stream], wp_far[...], ((0,), (0,)))
+        arrived(att_far.at[0, stream], a_recv.at[0, stream], pair)
+        total = branch[stream] + dot(att_far[0, stream], wp_far[...], ((0,), (0,)))
         branch[stream] = total * gate_ref[...].reshape(1, D)
 
         def mix_rows(n, carry):
@@ -300,7 +299,7 @@
             return carry
 
         lax.fori_loop(0, 8, mix_rows, 0, unroll=2)
-        qkv[0] = dot(wcq[...], normed[...], ((1,), (1,)))
+        asked[stream] = dot(wcq[...], normed[...], ((1,), (1,)))
 
     def cross(stream):
         row = lax.broadcasted_iota(jnp.int32, (TEXT_ROWS, FRAMES), 0)
@@ -309,32 +308,26 @@
             low, high = head * HD, (head + 1) * HD
             start, end = low // 128 * 128, min(-(-high // 128) * 128, WIDTH)
             place = lax.broadcasted_iota(jnp.int32, (end - start, FRAMES), 0) + start
-            query = jnp.where((place >= low) & (place < high), qkv[0, start:end], 0.0).astype(jnp.bfloat16)
+            query = jnp.where((place >= low) & (place < high), asked[stream, start:end], 0.0).astype(jnp.bfloat16)
             return dot(tk[:, start:end], query, ((1,), (0,)))
 
         def value_of(head):
             return tv[head * HD : (head + 1) * HD, :TEXT_ROWS].astype(jnp.bfloat16)
 
         attend(scores_of, value_of, row < length_ref[0], att.at[1, stream])
-        partial[...] = dot(att[1, stream], wcp[...], ((0,), (0,)))
-
-        def fold_partial(n, carry):
-            give[stream, n] = fold(partial[rows_of(n, 8)]).astype(jnp.bfloat16)
-            return carry
-
-        lax.fori_loop(0, NQ, fold_partial, 0, unroll=2)
-        send(give.at[stream], taken.at[stream], a_send.at[1, stream], a_recv.at[1, stream], pair)
+        send(att.at[1, stream], att_far.at[1, stream], a_send.at[1, stream], a_recv.at[1, stream], pair)
+        partial[stream] = dot(att[1, stream], wcp[...], ((0,), (0,)))
 
     def fold(rows):
         high = jnp.concatenate([rows[:, LOW:], jnp.zeros((8, LOW - HIGH), jnp.float32)], axis=1)
         return jnp.concatenate([rows[:, :LOW], high], axis=0)
 
     def out2_add(stream):
-        arrived(taken.at[stream], a_recv.at[1, stream], pair)
+        arrived(att_far.at[1, stream], a_recv.at[1, stream], pair)
+        partial[stream] += dot(att_far[1, stream], wcp_far[...], ((0,), (0,)))
 
         def add_rows(n, carry):
-            both = give[stream, n].astype(jnp.float32) + taken[stream, n].astype(jnp.float32)
-            om[stream, n] = (fold(branch[stream, rows_of(n, 8)]) + both).astype(jnp.bfloat16)
+            om[stream, n] = fold(branch[stream, rows_of(n, 8)] + partial[stream, rows_of(n, 8)]).astype(jnp.bfloat16)
             return carry
 
         lax.fori_loop(0, NQ, add_rows, 0, unroll=2)
@@ -386,14 +379,15 @@
 
     text_products()
     pl.semaphore_wait(barrier, NZ - 1 + NQ - 1 + 1)
+    text_send()
     in1_send(0)
-    text_send()
     send(wp_hbm.at[half_rows], wp_far.at[half_rows], w_send.at[0], w_recv.at[0], pair)
     in1_send(1)
+    send(wcp_hbm.at[quarter_rows], wcp_far.at[quarter_rows], w_send.at[2], w_recv.at[2], pair)
     text_core_sum()
-    text_x_sum()
     in1_done(0)
     in2_send(0)
+    text_x_sum()
     in1_done(1)
     in2_send(1)
     text_z_sum()
@@ -402,26 +396,30 @@
     in2_done(0)
     temporal_norm(0)
     loads[5].wait()
-    text_y_sum()
     temporal(0)
+    text_z_gather()
     arrived(wp_far.at[half_rows], w_recv.at[0], pair)
     send(wp_far.at[half_rows], wp_far.at[half_rows], w_send.at[1], w_recv.at[1], sibling)
-    text_z_gather()
     in2_done(1)
     temporal_norm(1)
+    temporal(1)
+    arrived(wcp_far.at[quarter_rows], w_recv.at[2], pair)
+    send(wcp_far.at[quarter_rows], wcp_far.at[quarter_rows], w_send.at[4], w_recv.at[4], beside)
     text_x_gather()
-    temporal(1)
     loads[6].wait()
     loads[7].wait()
     arrived(wp_far.at[other_rows], w_recv.at[1], sibling)
-    text_core_gather()
     mix(0)
     loads[8].wait()
+    text_core_gather()
     cross(0)
+    arrived(wcp_far.at[beside_rows], w_recv.at[4], beside)
+    send(wcp_far.at[half_rows], wcp_far.at[half_rows], w_send.at[3], w_recv.at[3], sibling)
     mix(1)
-    cross(1)
+    arrived(wcp_far.at[other_rows], w_recv.at[3], sibling)
     out2_add(0)
     out2_send(0)
+    cross(1)
     out2_add(1)
     out2_send(1)
     out2_done(0)
@@ -445,21 +443,20 @@
             vmem((D,), f32), vmem((D,), f32), vmem((D,), f32),
             vmem((2, 32, WIDTH), bf16), vmem((32, TEXT_LEN), bf16),
             vmem((3, WIDTH, D), bf16), vmem((WIDTH, D), bf16), vmem((WIDTH, D), bf16),
-            vmem((WIDTH, D), bf16), vmem((WIDTH, D), bf16),
+            vmem((WIDTH, D), bf16), vmem((WIDTH, D), bf16), vmem((WIDTH, D), bf16),
             vmem((NZ, 2, 16, D), bf16), vmem((128, 128), f32), vmem((128, 128), f32), vmem((256, 128), f32),
             vmem((2, NQ, 16, LOW), bf16), vmem((2, NQ, 16, LOW), bf16),
-            vmem((FRAMES, D), bf16), vmem((3, WIDTH, FRAMES), f32),
-            vmem((2, 2, WIDTH, FRAMES), bf16), vmem((2, WIDTH, FRAMES), bf16),
-            vmem((2, FRAMES, D), f32), vmem((FRAMES, D), f32),
-            vmem((2, NQ, 16, LOW), bf16), vmem((2, NQ, 16, LOW), bf16),
+            vmem((FRAMES, D), bf16), vmem((3, WIDTH, FRAMES), f32), vmem((2, WIDTH, FRAMES), f32),
+            vmem((2, 2, WIDTH, FRAMES), bf16), vmem((2, 2, WIDTH, FRAMES), bf16),
+            vmem((2, FRAMES, D), f32), vmem((2, FRAMES, D), f32),
             vmem((2, NQ, 16, LOW), bf16), vmem((2, NQ, 16, LOW), bf16), vmem((2, NZ, 16, D), bf16),
             vmem((32, 384), bf16), vmem((192, 16, 128), bf16), vmem((96, 16, 128), bf16), vmem((96, 16, 128), bf16),
-            vmem((4, 24, 16, 128), bf16), vmem((24, 16, 128), bf16), vmem((8, 3, 16, 128), bf16),
-            vmem((3, 16, 128), bf16), vmem((3, 16, 128), bf16), vmem((192, 16, 128), bf16),
+            vmem((8, 12, 16, 128), bf16), vmem((24, 8, 128), f32), vmem((8, 3, 8, 128), f32), vmem((24, 8, 128), f32),
+            vmem((192, 16, 128), bf16),
             vmem((TEXT_ROWS, WIDTH), bf16), vmem((640, 384), f32),
-            dma((9,)), dma((2,)), dma((2,)), dma((7, 2)), dma((8, 2)), dma((2, 16)), dma((2, 16)),
+            dma((9,)), dma((6,)), dma((6,)), dma((7, 2)), dma((8, 2)), dma((2, 16)), dma((2, 16)),
             dma((2, 2)), dma((2, 2)), dma((2, 16)), dma((2, 16)), dma((7, 2)), dma((8, 2)),
-            dma((2,)), dma((2,)), dma((2, 4)), dma((2, 4)), dma((2, 8)), dma((2, 8)), dma((1,)), dma((1,)), dma((4,)),
+            dma((2,)), dma((2,)), dma((2, 8)), dma((2, 8)), dma((2, 8)), dma((2, 8)), dma((4,)),
         ],
         compiler_params=pltpu.CompilerParams(
             collective_id=0, has_side_effects=True, vmem_limit_bytes=60 * 1024 * 1024

time: 83.3 us -> 75.6 us (0.908)
  Pallas kernels: 80.3 us -> 72.5 us
    pallas_call x1, Pallas kernels: 80.3 us -> 72.5 us  [mega(): pl.pallas_call(kernel, out_shape=jax.ShapeDtypeStruct((TOKENS, D), bf16),...]
where the time goes in v6:
time: 75.6 us; the launch traced here: 75.4 us
  Pallas kernels  72.5 us (96%)
  other arithmetic  2.19 us (3%)
    pallas_call x1, Pallas kernels, mega(): pl.pallas_call(kernel, out_shape=jax.ShapeDtypeStruct((TOKENS, D), bf16),...  72.5 us
    add x1, other arithmetic, body(): video_latent.astype(jnp.float32)  2.19 us

profile of v6, /device:TPU:1, one launch (start us, length us, event | category | flops | bytes accessed | tf_op | source)
XLA Modules:
  0.0 75.4 jit_solution(14540806826652426205)
XLA Ops:
  0.7 0.0 copy-start
  0.7 72.5 %stdit.1 = bf16[256,1152]{1,0:T(8,128)(2,1)} custom-call(s32[1]{0:T(128)S(6)} %copy.12.length_ref, bf16[256,1152]{1,0:T(8,128)(2,1)} %bitcast.7, f32[1152]{0:T(1024)} %shift_hbm.1, f32[1152]{0:T(1024)} %scale_hbm.1, f32[1152]{0:T(1024)} %gate_hbm.1, bf16[3,576,1152]{2,1,0:T(8,128)(2,1)} %bitcast.8, bf16[576,1152]{1,0:T(8,128)(2,1)} %wp_hbm.1, ...), custom_call_target="tpu_custom_call" | custom-call | flops 4000000000 | bytes 12000000 | tf_op jit(solution)/shard_map/stdit/pallas_call | solution.py:437
  73.2 0.0 copy-done
  73.2 2.2 %convert_add_fusion = f32[1,256,1152]{2,1,0:T(8,128)} fusion(bf16[1,256,1152]{2,1,0:T(8,128)(2,1)S(1)} %copy-done, bf16[256,1152]{1,0:T(8,128)(2,1)} %stdit.1), kind=kLoop, calls=%fused_computation | loop fusion | flops 884736 | bytes 2359296 | tf_op jit(solution)/shard_map/add | solution.py:478
Async XLA Ops:
  0.7 72.5 %copy-start = (bf16[1,256,1152]{2,1,0:T(8,128)(2,1)S(1)}, bf16[1,256,1152]{2,1,0:T(8,128)(2,1)}, u32[]{:S(2)}) copy-start(bf16[1,256,1152]{2,1,0:T(8,128)(2,1)} %param.11) | copy-start | bytes 1769476

commit v7 on v6

--- a/solution.py
+++ b/solution.py
@@ -28,7 +28,7 @@
     return lax.dot_general(a, b, (dims, ((), ())), preferred_element_type=jnp.float32)
 
 
-def attend(scores_of, value_of, visible, target):
+def attend(scores_of, value_of, visible, target, after):
     for group in range(0, HEADS, 4):
         scores = [scores_of(head) for head in range(group, group + 4)]
         weights, totals = [], []
@@ -42,6 +42,7 @@
         mixed = [dot(value_of(group + n), weights[n], ((1,), (0,))) * totals[n] for n in range(4)]
         for n in (0, 2):
             target[(group + n) * HD : (group + n + 2) * HD] = jnp.concatenate(mixed[n : n + 2], axis=0).astype(jnp.bfloat16)
+        after(group // 4)
 
 
 def kernel(
@@ -208,6 +209,9 @@
     beside = at_q(q + 4 - 8 * odd_x)
     quarter_rows = pl.ds(pl.multiple_of(core * 288 + odd_x * 144, 16), 144)
     beside_rows = pl.ds(pl.multiple_of(core * 288 + 144 - odd_x * 144, 16), 144)
+    other_quarters = [
+        pl.ds(pl.multiple_of(288 - core * 288 + start, 16), 144) for start in (odd_x * 144, 144 - odd_x * 144)
+    ]
     other_rows = pl.ds(pl.multiple_of(288 - core * 288, 288), 288)
     own = []
 
@@ -283,13 +287,23 @@
         lax.fori_loop(0, 3, project, 0)
         attend(
             lambda head: dot(head_rows(1, head), head_rows(0, head), ((0,), (0,))),
-            lambda head: head_rows(2, head), None, att.at[0, stream],
+            lambda head: head_rows(2, head), None, att.at[0, stream], lambda half: swap(0, stream, half),
         )
-        send(att.at[0, stream], att_far.at[0, stream], a_send.at[0, stream], a_recv.at[0, stream], pair)
+
+    def swap(kind, stream, half):
+        rows = pl.ds(half * 288, 288)
+        send(
+            att.at[kind, stream, rows], att_far.at[kind, stream, rows],
+            a_send.at[kind, stream, half], a_recv.at[kind, stream, half], pair,
+        )
+
+    def swapped(kind, stream):
+        for half in range(2):
+            arrived(att_far.at[kind, stream, pl.ds(half * 288, 288)], a_recv.at[kind, stream, half], pair)
 
     def mix(stream):
         branch[stream] = dot(att[0, stream], wp[...], ((0,), (0,)))
-        arrived(att_far.at[0, stream], a_recv.at[0, stream], pair)
+        swapped(0, stream)
         total = branch[stream] + dot(att_far[0, stream], wp_far[...], ((0,), (0,)))
         branch[stream] = total * gate_ref[...].reshape(1, D)
 
@@ -314,8 +328,7 @@
         def value_of(head):
             return tv[head * HD : (head + 1) * HD, :TEXT_ROWS].astype(jnp.bfloat16)
 
-        attend(scores_of, value_of, row < length_ref[0], att.at[1, stream])
-        send(att.at[1, stream], att_far.at[1, stream], a_send.at[1, stream], a_recv.at[1, stream], pair)
+        attend(scores_of, value_of, row < length_ref[0], att.at[1, stream], lambda half: swap(1, stream, half))
         partial[stream] = dot(att[1, stream], wcp[...], ((0,), (0,)))
 
     def fold(rows):
@@ -323,7 +336,7 @@
         return jnp.concatenate([rows[:, :LOW], high], axis=0)
 
     def out2_add(stream):
-        arrived(att_far.at[1, stream], a_recv.at[1, stream], pair)
+        swapped(1, stream)
         partial[stream] += dot(att_far[1, stream], wcp_far[...], ((0,), (0,)))
 
         def add_rows(n, carry):
@@ -334,9 +347,14 @@
 
     def out2_send(stream):
         place = place_of(q)
-        for step in (8, 4, 12, 10, 6, 14, 2, 9, 5, 13, 11, 7, 15, 3, 1):
-            dest = lax.rem(q + step, NQ)
-            send(om.at[stream, dest], o2.at[stream, place], o2_send.at[stream, step], o2_recv.at[stream, place], at_q(dest))
+        for first in range(2):
+            for step in (4, 6, 2, 5, 3, 7, 1, 0):
+                dest = 2 * lax.rem(spot + step, 8) + first
+                when = None if step else core != first
+                send(
+                    om.at[stream, dest], o2.at[stream, place],
+                    o2_send.at[stream, first * 8 + step], o2_recv.at[stream, place], at_q(dest), when,
+                )
         o2[stream, place] = om[stream, q]
 
     def out2_done(stream):
@@ -402,9 +420,10 @@
     send(wp_far.at[half_rows], wp_far.at[half_rows], w_send.at[1], w_recv.at[1], sibling)
     in2_done(1)
     temporal_norm(1)
-    temporal(1)
     arrived(wcp_far.at[quarter_rows], w_recv.at[2], pair)
     send(wcp_far.at[quarter_rows], wcp_far.at[quarter_rows], w_send.at[4], w_recv.at[4], beside)
+    send(wcp_far.at[quarter_rows], wcp_far.at[quarter_rows], w_send.at[3], w_recv.at[3], sibling)
+    temporal(1)
     text_x_gather()
     loads[6].wait()
     loads[7].wait()
@@ -414,9 +433,10 @@
     text_core_gather()
     cross(0)
     arrived(wcp_far.at[beside_rows], w_recv.at[4], beside)
-    send(wcp_far.at[half_rows], wcp_far.at[half_rows], w_send.at[3], w_recv.at[3], sibling)
+    send(wcp_far.at[beside_rows], wcp_far.at[beside_rows], w_send.at[5], w_recv.at[5], sibling)
     mix(1)
-    arrived(wcp_far.at[other_rows], w_recv.at[3], sibling)
+    for n in (3, 5):
+        arrived(wcp_far.at[other_quarters[n // 4]], w_recv.at[n], sibling)
     out2_add(0)
     out2_send(0)
     cross(1)
@@ -455,7 +475,7 @@
             vmem((192, 16, 128), bf16),
             vmem((TEXT_ROWS, WIDTH), bf16), vmem((640, 384), f32),
             dma((9,)), dma((6,)), dma((6,)), dma((7, 2)), dma((8, 2)), dma((2, 16)), dma((2, 16)),
-            dma((2, 2)), dma((2, 2)), dma((2, 16)), dma((2, 16)), dma((7, 2)), dma((8, 2)),
+            dma((2, 2, 2)), dma((2, 2, 2)), dma((2, 16)), dma((2, 16)), dma((7, 2)), dma((8, 2)),
             dma((2,)), dma((2,)), dma((2, 8)), dma((2, 8)), dma((2, 8)), dma((2, 8)), dma((4,)),
         ],
         compiler_params=pltpu.CompilerParams(

time: 75.6 us -> 75.2 us (level)
  no operation moved by 1% of the time
where the time goes in v7:
time: 75.2 us; the launch traced here: 75 us
  Pallas kernels  72.1 us (96%)
  other arithmetic  2.19 us (3%)
    pallas_call x1, Pallas kernels, mega(): pl.pallas_call(kernel, out_shape=jax.ShapeDtypeStruct((TOKENS, D), bf16),...  72.1 us
    add x1, other arithmetic, body(): video_latent.astype(jnp.float32)  2.19 us

profile of v7, /device:TPU:1, one launch (start us, length us, event | category | flops | bytes accessed | tf_op | source)
XLA Modules:
  0.0 75.0 jit_solution(3185792835883297186)
XLA Ops:
  0.7 0.0 copy-start
  0.7 72.1 %stdit.1 = bf16[256,1152]{1,0:T(8,128)(2,1)} custom-call(s32[1]{0:T(128)S(6)} %copy.12.length_ref, bf16[256,1152]{1,0:T(8,128)(2,1)} %bitcast.7, f32[1152]{0:T(1024)} %shift_hbm.1, f32[1152]{0:T(1024)} %scale_hbm.1, f32[1152]{0:T(1024)} %gate_hbm.1, bf16[3,576,1152]{2,1,0:T(8,128)(2,1)} %bitcast.8, bf16[576,1152]{1,0:T(8,128)(2,1)} %wp_hbm.1, ...), custom_call_target="tpu_custom_call" | custom-call | flops 4000000000 | bytes 12000000 | tf_op jit(solution)/shard_map/stdit/pallas_call | solution.py:457
  72.8 0.0 copy-done
  72.8 2.2 %convert_add_fusion = f32[1,256,1152]{2,1,0:T(8,128)} fusion(bf16[1,256,1152]{2,1,0:T(8,128)(2,1)S(1)} %copy-done, bf16[256,1152]{1,0:T(8,128)(2,1)} %stdit.1), kind=kLoop, calls=%fused_computation | loop fusion | flops 884736 | bytes 2359296 | tf_op jit(solution)/shard_map/add | solution.py:498
Async XLA Ops:
  0.7 72.1 %copy-start = (bf16[1,256,1152]{2,1,0:T(8,128)(2,1)S(1)}, bf16[1,256,1152]{2,1,0:T(8,128)(2,1)}, u32[]{:S(2)}) copy-start(bf16[1,256,1152]{2,1,0:T(8,128)(2,1)} %param.11) | copy-start | bytes 1769476

commit v8 on v7

--- a/solution.py
+++ b/solution.py
@@ -81,6 +81,13 @@
     pair = (z * NQ + other_y(q), 1 - hi)
     sibling = at_q(q + 1 - 2 * core)
 
+    barrier = pltpu.get_barrier_semaphore()
+    for step in range(1, NZ):
+        pl.semaphore_signal(barrier, inc=1, device_id=at_z(lax.rem(z + step, NZ)), device_id_type=MESH)
+    for step in range(1, NQ):
+        pl.semaphore_signal(barrier, inc=1, device_id=at_q(lax.rem(q + step, NQ)), device_id_type=MESH)
+    pl.semaphore_signal(barrier, inc=1, device_id=pair, device_id_type=MESH)
+
     loads = [
         pltpu.make_async_copy(source, target, load_sem.at[n])
         for n, (source, target) in enumerate(
@@ -92,13 +99,6 @@
     ]
     for load in loads:
         load.start()
-
-    barrier = pltpu.get_barrier_semaphore()
-    for step in range(1, NZ):
-        pl.semaphore_signal(barrier, inc=1, device_id=at_z(lax.rem(z + step, NZ)), device_id_type=MESH)
-    for step in range(1, NQ):
-        pl.semaphore_signal(barrier, inc=1, device_id=at_q(lax.rem(q + step, NQ)), device_id_type=MESH)
-    pl.semaphore_signal(barrier, inc=1, device_id=pair, device_id_type=MESH)
 
     def remote(source, target, send, recv, device):
         return pltpu.make_async_remote_copy(
@@ -414,8 +414,8 @@
     in2_done(0)
     temporal_norm(0)
     loads[5].wait()
+    text_z_gather()
     temporal(0)
-    text_z_gather()
     arrived(wp_far.at[half_rows], w_recv.at[0], pair)
     send(wp_far.at[half_rows], wp_far.at[half_rows], w_send.at[1], w_recv.at[1], sibling)
     in2_done(1)

time: 75.2 us -> 74.4 us (0.989)
  no operation moved by 1% of the time
where the time goes in v8:
time: 74.4 us; the launch traced here: 74.2 us
  Pallas kernels  71.4 us (96%)
  other arithmetic  2.19 us (3%)
    pallas_call x1, Pallas kernels, mega(): pl.pallas_call(kernel, out_shape=jax.ShapeDtypeStruct((TOKENS, D), bf16),...  71.4 us
    add x1, other arithmetic, body(): video_latent.astype(jnp.float32)  2.19 us

profile of v8, /device:TPU:1, one launch (start us, length us, event | category | flops | bytes accessed | tf_op | source)
XLA Modules:
  0.0 74.2 jit_solution(15039754113558840229)
XLA Ops:
  0.7 0.0 copy-start
  0.7 71.4 %stdit.1 = bf16[256,1152]{1,0:T(8,128)(2,1)} custom-call(s32[1]{0:T(128)S(6)} %copy.12.length_ref, bf16[256,1152]{1,0:T(8,128)(2,1)} %bitcast.7, f32[1152]{0:T(1024)} %shift_hbm.1, f32[1152]{0:T(1024)} %scale_hbm.1, f32[1152]{0:T(1024)} %gate_hbm.1, bf16[3,576,1152]{2,1,0:T(8,128)(2,1)} %bitcast.8, bf16[576,1152]{1,0:T(8,128)(2,1)} %wp_hbm.1, ...), custom_call_target="tpu_custom_call" | custom-call | flops 4000000000 | bytes 12000000 | tf_op jit(solution)/shard_map/stdit/pallas_call | solution.py:457
  72.0 0.0 copy-done
  72.0 2.2 %convert_add_fusion = f32[1,256,1152]{2,1,0:T(8,128)} fusion(bf16[1,256,1152]{2,1,0:T(8,128)(2,1)S(1)} %copy-done, bf16[256,1152]{1,0:T(8,128)(2,1)} %stdit.1), kind=kLoop, calls=%fused_computation | loop fusion | flops 884736 | bytes 2359296 | tf_op jit(solution)/shard_map/add | solution.py:498
Async XLA Ops:
  0.7 71.4 %copy-start = (bf16[1,256,1152]{2,1,0:T(8,128)(2,1)S(1)}, bf16[1,256,1152]{2,1,0:T(8,128)(2,1)}, u32[]{:S(2)}) copy-start(bf16[1,256,1152]{2,1,0:T(8,128)(2,1)} %param.11) | copy-start | bytes 1769476
